TPU v7x, 128 devices: a whole 4x4x4 slice. The times are simulated.
128 devices in a mesh: expert: 8 (over y_hi, x), tensor: 16 (over z, y_lo, core).
Axes of the slice: x: 4, y: 4 (y_hi: 2, y_lo: 2; y = y_hi * 2 + y_lo), z: 4, core: 2. Of those that a mesh axis runs over, the one named last changes fastest.
Arguments:
- hidden_in: bfloat16 [16384, 3584], P(('expert', 'tensor')), may hold values from -50 to 50
- norm_gain: float32 [3584], replicated, may hold values from 0.1 to 1.9
- upstream: bfloat16 [16384, 3584], P(('expert', 'tensor')), may hold values from -20 to 20
- routes: int32 [16384, 4], P(('expert', 'tensor')), may hold values from 0 to 127, all different within a row; in each aligned block of 128 rows (0 to 127, 128 to 255, ...) at most 6 rows name the same one
- combine_fixed: int32 [16384, 4], P(('expert', 'tensor')), may hold values from 6554 to 65535
- w_gate: bfloat16 [128, 3584, 1024], P(('expert', 'tensor')), may hold values from -0.09375 to 0.09375
- w_up: bfloat16 [128, 3584, 1024], P(('expert', 'tensor')), may hold values from -0.09375 to 0.09375
- w_down: bfloat16 [128, 1024, 3584], P(('expert', 'tensor')), may hold values from -0.1875 to 0.1875
Outputs:
- input_grad: bfloat16 [16384, 3584], P(('expert', 'tensor'))
- gain_grad: float32 [3584], replicated
- combine_grad: bfloat16 [16384, 4], P(('expert', 'tensor'))
Inputs may be any that keep to these rules, and one draw needn't show every extreme that they name: `routes`: each row names 4 different experts. Among the 128 rows of one device no expert is named by more than 6 rows, and in every draw some expert is named by exactly 6 rows of some device.
All inputs are finite; a program needn't handle non-finite values.
Results may differ from a plain program's by a relative error of at most 0.0071.
Values may be sent and summed in bfloat16 or wider, within the bound.
A program may use at most 128 MiB of HBM per device.

v0:
```python
import jax
import jax.numpy as jnp
from jax import lax
from jax.sharding import PartitionSpec as P

CONTRACT = (((1,), (1,)), ((), ()))


def recompute(rows_in, weight_gate, weight_up):
    gate_pre = jnp.dot(rows_in, weight_gate, preferred_element_type=jnp.float32)
    up_pre = jnp.dot(rows_in, weight_up, preferred_element_type=jnp.float32)
    return (gate_pre, up_pre)


def finish(gate_pre, up_pre, grads_in, scale_in, weight_gate, weight_up, weight_down):
    back_proj = lax.dot_general(grads_in, weight_down, CONTRACT, preferred_element_type=jnp.float32)
    gate_sig = jax.nn.sigmoid(gate_pre)
    gate_act = gate_pre * gate_sig
    comb_grad = jnp.sum(gate_act * up_pre * back_proj, axis=1).astype(jnp.bfloat16)
    scaled = scale_in.astype(jnp.float32)[:, None] * back_proj
    d_gate = (scaled * up_pre * gate_sig * (1.0 + gate_pre * (1.0 - gate_sig))).astype(jnp.bfloat16)
    d_up = (scaled * gate_act).astype(jnp.bfloat16)
    slot_grad = lax.dot_general(d_gate, weight_gate, CONTRACT, preferred_element_type=jnp.float32)
    slot_grad = slot_grad + lax.dot_general(
        d_up, weight_up, CONTRACT, preferred_element_type=jnp.float32
    )
    return (slot_grad.astype(jnp.bfloat16), comb_grad)


def shards(hidden_in, norm_gain, upstream, routes, combine_fixed, w_gate, w_up, w_down):
    tok_rows, model_width = hidden_in.shape
    top_count = routes.shape[1]
    expert_count = lax.axis_size("expert")
    tensor_count = lax.axis_size("tensor")
    experts = expert_count * tensor_count
    capacity = 3 * tok_rows * top_count // (2 * experts)
    total_rows = experts * capacity
    hidden_f = hidden_in.astype(jnp.float32)
    inv_rms = lax.rsqrt(jnp.mean(hidden_f * hidden_f, axis=1, keepdims=True) + 1e-06)
    unit_rows = hidden_f * inv_rms
    normed = (unit_rows * norm_gain[None, :]).astype(jnp.bfloat16)
    weight = (combine_fixed.astype(jnp.float32) / 65536.0).astype(jnp.bfloat16)
    flat_routes = routes.reshape(-1)
    onehot = (flat_routes[:, None] == jnp.arange(experts, dtype=jnp.int32)[None, :]).astype(
        jnp.int32
    )
    position = jnp.sum((jnp.cumsum(onehot, axis=0) - 1) * onehot, axis=1)
    slot_index = flat_routes * capacity + position
    token_of = jnp.arange(tok_rows * top_count, dtype=jnp.int32) // top_count
    rows_send = (
        jnp.zeros((total_rows, model_width), jnp.bfloat16).at[slot_index].set(normed[token_of])
    )
    grads_send = (
        jnp.zeros((total_rows, model_width), jnp.bfloat16).at[slot_index].set(upstream[token_of])
    )
    scale_send = jnp.zeros((total_rows,), jnp.bfloat16).at[slot_index].set(weight.reshape(-1))
    weight_gate = w_gate[0]
    weight_up = w_up[0]
    weight_down = w_down[0]
    slab_shape = (experts, capacity)
    rows_send = rows_send.reshape(slab_shape + (model_width,))
    grads_send = grads_send.reshape(slab_shape + (model_width,))
    scale_send = scale_send.reshape(slab_shape)
    rows_recv, grads_recv, scale_recv = (
        lax.all_to_all(rows_send, ("expert", "tensor"), split_axis=0, concat_axis=0, tiled=True),
        lax.all_to_all(grads_send, ("expert", "tensor"), split_axis=0, concat_axis=0, tiled=True),
        lax.all_to_all(scale_send, ("expert", "tensor"), split_axis=0, concat_axis=0, tiled=True),
    )
    gate_pre, up_pre = recompute(rows_recv.reshape(total_rows, model_width), weight_gate, weight_up)
    slot_grad, comb_grad = finish(
        gate_pre,
        up_pre,
        grads_recv.reshape(total_rows, model_width),
        scale_recv.reshape(total_rows),
        weight_gate,
        weight_up,
        weight_down,
    )
    slot_grad = slot_grad.reshape(slab_shape + (model_width,))
    comb_grad = comb_grad.reshape(slab_shape)
    slot_back, comb_back = (
        lax.all_to_all(slot_grad, ("expert", "tensor"), split_axis=0, concat_axis=0, tiled=True),
        lax.all_to_all(comb_grad, ("expert", "tensor"), split_axis=0, concat_axis=0, tiled=True),
    )
    slot_back = slot_back.reshape(total_rows, model_width)
    comb_back = comb_back.reshape(total_rows)
    picked = slot_back[slot_index].reshape(tok_rows, top_count, model_width)
    normed_grad = jnp.sum(picked.astype(jnp.float32), axis=1)
    combine_grad = comb_back[slot_index].reshape(tok_rows, top_count)
    gain_part = jnp.sum(normed_grad * unit_rows, axis=0)
    gain_grad = lax.psum(gain_part, ("expert", "tensor"))
    scaled_grad = normed_grad * norm_gain[None, :]
    project = jnp.mean(scaled_grad * unit_rows, axis=1, keepdims=True)
    input_grad = (inv_rms * (scaled_grad - unit_rows * project)).astype(jnp.bfloat16)
    return (input_grad, gain_grad, combine_grad)


def solution(mesh):
    in_specs = (
        P(("expert", "tensor"), None),
        P(),
        P(("expert", "tensor"), None),
        P(("expert", "tensor"), None),
        P(("expert", "tensor"), None),
        P(("expert", "tensor"), None, None),
        P(("expert", "tensor"), None, None),
        P(("expert", "tensor"), None, None),
    )
    out_specs = (P(("expert", "tensor"), None), P(), P(("expert", "tensor"), None))
    return jax.shard_map(shards, mesh=mesh, in_specs=in_specs, out_specs=out_specs, check_vma=False)
```

profile of v0, /device:TPU:0, one launch (start us, length us, event | category | flops | bytes accessed | tf_op | source)
XLA Modules:
  0.0 542.0 jit_solution(5063906100194521129)
XLA Ops:
  0.7 0.9 copy.19
  1.8 0.7 broadcast_multiply_fusion
  2.5 0.1 copy.21
  2.6 0.2 fusion.35
  3.0 0.1 copy.18
  3.2 0.7 multiply_convert_fusion.4
  3.9 0.1 copy.23
  4.0 0.1 reshape.217
  4.1 0.2 fusion.34
  4.4 3.8 scatter_custom_fusion
  8.1 0.8 all_to_all.25
  8.9 11.3 %all-to-all-start = ((bf16[128,1,6]{2,1,0:T(2,128)(2,1)}), bf16[128,1,6]{2,1,0:T(2,128)(2,1)S(1)}, u32[]{:S(2)}, u32[]{:S(2)}) async-start(bf16[128,1,6]{2,1,0:T(2,128)(2,1)} %all_to_all.25), calls=%async_computation | async-start | bytes 131072 | tf_op jit(solution)/shard_map/all_to_all | solution.py:67
  20.3 1.4 fusion.29
  21.8 0.3 fusion.23
  22.1 19.8 %scatter_custom_fusion.2 = bf16[768,3584]{1,0:T(8,128)(2,1)} fusion(s32[512]{0:T(512)S(1)} %bitcast.33, bf16[128,3584]{1,0:T(8,128)(2,1)S(1)} %fusion.23, s32[1024]{0:T(1024)S(1)} %pad_clamp_fusion.1, bf16[]{:T(256)} %constant.37.clone.1), kind=kCustom, calls=%fused_computation.18 | custom fusion | bytes 5505026 | tf_op jit(solution)/shard_map/scatter | solution.py:51
  41.8 9.6 %reshape.173 = bf16[128,6,3584]{2,1,0:T(8,128)(2,1)} reshape(bf16[768,3584]{1,0:T(8,128)(2,1)} %scatter_custom_fusion.2) | data formatting | bytes 11010048 | tf_op jit(solution)/shard_map/reshape | solution.py:61
  51.4 10.6 %all-to-all-start.2 = ((bf16[128,6,3584]{2,1,0:T(8,128)(2,1)}), bf16[128,6,3584]{2,1,0:T(8,128)(2,1)}, u32[]{:S(2)}, u32[]{:S(2)}) async-start(bf16[128,6,3584]{2,1,0:T(8,128)(2,1)} %reshape.173), calls=%async_computation.2 | async-start | bytes 14680064 | tf_op jit(solution)/shard_map/all_to_all | solution.py:65
  62.0 19.7 %scatter_custom_fusion.1 = bf16[768,3584]{1,0:T(8,128)(2,1)} fusion(s32[512]{0:T(512)S(1)} %bitcast.34, bf16[128,3584]{1,0:T(8,128)(2,1)S(1)} %copy-done, s32[1024]{0:T(1024)S(1)} %pad_clamp_fusion.1, bf16[]{:T(256)} %constant.37.clone.1), kind=kCustom, calls=%fused_computation.20 | custom fusion | bytes 5505026 | tf_op jit(solution)/shard_map/scatter | solution.py:54
  81.8 9.6 %reshape.171 = bf16[128,6,3584]{2,1,0:T(8,128)(2,1)} reshape(bf16[768,3584]{1,0:T(8,128)(2,1)} %scatter_custom_fusion.1) | data formatting | bytes 11010048 | tf_op jit(solution)/shard_map/reshape | solution.py:62
  91.4 61.3 %all-to-all-done.2 = bf16[128,6,3584]{2,1,0:T(8,128)(2,1)} async-done(((bf16[128,6,3584]{2,1,0:T(8,128)(2,1)}), bf16[128,6,3584]{2,1,0:T(8,128)(2,1)}, u32[]{:S(2)}, u32[]{:S(2)}) %all-to-all-start.2) | async-done | bytes 5505056 | tf_op jit(solution)/shard_map/all_to_all | solution.py:65
  152.7 13.3 %all-to-all-start.1 = ((bf16[128,6,3584]{2,1,0:T(8,128)(2,1)}), bf16[128,6,3584]{2,1,0:T(8,128)(2,1)}, u32[]{:S(2)}, u32[]{:S(2)}) async-start(bf16[128,6,3584]{2,1,0:T(8,128)(2,1)} %reshape.171), calls=%async_computation.1 | async-start | bytes 14680064 | tf_op jit(solution)/shard_map/all_to_all | solution.py:66
  165.9 0.2 convert_reduce_fusion
  166.1 0.1 reshape.179
  166.3 9.7 %reshape.174 = bf16[768,3584]{1,0:T(8,128)(2,1)} reshape(bf16[128,6,3584]{2,1,0:T(8,128)(2,1)} %all-to-all-done.2) | data formatting | bytes 11010048 | tf_op jit(solution)/shard_map/reshape | solution.py:69
  176.0 11.9 %fusion.2 = f32[768,1024]{1,0:T(8,128)} fusion(bf16[768,3584]{1,0:T(8,128)(2,1)} %reshape.174, bf16[1,3584,1024]{2,1,0:T(8,128)(2,1)} %param.13), kind=kOutput, calls=%fused_computation.10 | convolution fusion | flops 5637144576 | bytes 15990784 | tf_op jit(solution)/shard_map/dot_general | solution.py:10
  187.8 9.2 %fusion.6 = f32[768,1024]{1,0:T(8,128)} fusion(bf16[768,3584]{1,0:T(8,128)(2,1)S(1)} %copy-done.4, bf16[1,3584,1024]{2,1,0:T(8,128)(2,1)} %param.14), kind=kOutput, calls=%fused_computation.14 | convolution fusion | flops 5637144576 | bytes 15990784 | tf_op jit(solution)/shard_map/dot_general | solution.py:11
  197.1 59.0 %all-to-all-done.1 = bf16[128,6,3584]{2,1,0:T(8,128)(2,1)} async-done(((bf16[128,6,3584]{2,1,0:T(8,128)(2,1)}), bf16[128,6,3584]{2,1,0:T(8,128)(2,1)}, u32[]{:S(2)}, u32[]{:S(2)}) %all-to-all-start.1) | async-done | bytes 5505056 | tf_op jit(solution)/shard_map/all_to_all | solution.py:66
  256.0 9.7 %reshape.172 = bf16[768,3584]{1,0:T(8,128)(2,1)} reshape(bf16[128,6,3584]{2,1,0:T(8,128)(2,1)} %all-to-all-done.1) | data formatting | bytes 11010048 | tf_op jit(solution)/shard_map/reshape | solution.py:73
  265.7 12.7 %multiply_reduce_fusion = (bf16[768]{0:T(1024)(128)(2,1)S(1)}, f32[768,1024]{1,0:T(8,128)}) fusion(f32[768,1024]{1,0:T(8,128)} %fusion.6, f32[768,1024]{1,0:T(8,128)} %fusion.2, bf16[768,3584]{1,0:T(8,128)(2,1)} %reshape.172, bf16[1,1024,3584]{2,1,0:T(8,128)(2,1)} %param.15), kind=kOutput, calls=%fused_computation.22 | convolution fusion | flops 5642648576 | bytes 22283776 | tf_op jit(solution)/shard_map/dot_general | solution.py:16
  278.4 0.8 convert_element_type.76
  279.2 13.6 %all-to-all-start.4 = ((bf16[128,1,6]{2,1,0:T(2,128)(2,1)}), bf16[128,1,6]{2,1,0:T(2,128)(2,1)S(1)}, u32[]{:S(2)}, u32[]{:S(2)}) async-start(bf16[128,1,6]{2,1,0:T(2,128)(2,1)} %convert_element_type.76), calls=%async_computation.4 | async-start | bytes 131072 | tf_op jit(solution)/shard_map/all_to_all | solution.py:83
  292.8 16.2 %fusion = f32[768,3584]{1,0:T(8,128)} fusion(bf16[1,3584,1024]{2,1,0:T(8,128)(2,1)} %param.13, f32[768,1024]{1,0:T(8,128)} %fusion.2, f32[768,1024]{1,0:T(8,128)} %fusion.6, f32[768,1024]{1,0:T(8,128)} %get-tuple-element.12, f32[768]{0:T(1024)S(1)} %reshape.179), kind=kOutput, calls=%fused_computation.8 | convolution fusion | flops 5645795328 | bytes 27790336 | tf_op jit(solution)/shard_map/dot_general | solution.py:23
  309.0 13.2 %add_convert_fusion = bf16[768,3584]{1,0:T(8,128)(2,1)} fusion(f32[768,3584]{1,0:T(8,128)} %fusion, bf16[1,3584,1024]{2,1,0:T(8,128)(2,1)} %param.14, f32[768,1024]{1,0:T(8,128)S(1)} %copy-done.7, f32[768]{0:T(1024)S(1)} %reshape.179, f32[768,1024]{1,0:T(8,128)S(1)} %copy-done.6), kind=kOutput, calls=%fused_computation.7 | convolution fusion | flops 5648154624 | bytes 30149632 | tf_op jit(solution)/shard_map/dot_general | solution.py:24
  322.2 9.6 %reshape.175 = bf16[128,6,3584]{2,1,0:T(8,128)(2,1)} reshape(bf16[768,3584]{1,0:T(8,128)(2,1)} %add_convert_fusion) | data formatting | bytes 11010048 | tf_op jit(solution)/shard_map/reshape | solution.py:79
  331.7 10.6 %all-to-all-start.3 = ((bf16[128,6,3584]{2,1,0:T(8,128)(2,1)}), bf16[128,6,3584]{2,1,0:T(8,128)(2,1)}, u32[]{:S(2)}, u32[]{:S(2)}) async-start(bf16[128,6,3584]{2,1,0:T(8,128)(2,1)} %reshape.175), calls=%async_computation.3 | async-start | bytes 14680064 | tf_op jit(solution)/shard_map/all_to_all | solution.py:82
  342.4 0.2 reduce.1
  342.6 0.1 reshape.177
  342.7 3.5 gather_fusion.1
  346.2 0.1 reshape.178
  346.4 0.7 copy.26
  347.0 85.5 %all-to-all-done.3 = bf16[128,6,3584]{2,1,0:T(8,128)(2,1)} async-done(((bf16[128,6,3584]{2,1,0:T(8,128)(2,1)}), bf16[128,6,3584]{2,1,0:T(8,128)(2,1)}, u32[]{:S(2)}, u32[]{:S(2)}) %all-to-all-start.3) | async-done | bytes 5505056 | tf_op jit(solution)/shard_map/all_to_all | solution.py:82
  432.5 9.7 %reshape.176 = bf16[768,3584]{1,0:T(8,128)(2,1)} reshape(bf16[128,6,3584]{2,1,0:T(8,128)(2,1)} %all-to-all-done.3) | data formatting | bytes 11010048 | tf_op jit(solution)/shard_map/reshape | solution.py:85
  442.1 11.2 %gather_fusion = bf16[512,3584]{1,0:T(8,128)(2,1)} fusion(bf16[768,3584]{1,0:T(8,128)(2,1)} %reshape.176, s32[1024]{0:T(1024)S(1)} %pad_clamp_fusion), kind=kCustom, calls=%fused_computation.2 | custom fusion | bytes 7342080 | tf_op jit(solution)/shard_map/gather | solution.py:87
  453.3 7.5 %reshape.180 = f32[128,4,3584]{2,1,0:T(4,128)} reshape(bf16[512,3584]{1,0:T(8,128)(2,1)} %gather_fusion) | data formatting | bytes 11010048 | tf_op jit(solution)/shard_map/convert_element_type | solution.py:88
  460.8 7.5 %reduce_sum.59 = f32[128,3584]{1,0:T(8,128)S(1)} reduce(f32[128,4,3584]{2,1,0:T(4,128)} %reshape.180, f32[]{:T(128)} %constant.34.clone.1), dimensions={1}, to_apply=%region_7.8 | reduce | flops 1376256 | bytes 9175044 | tf_op jit(solution)/shard_map/reduce_sum | solution.py:88
  468.3 1.9 fusion.28
  470.2 1.4 fusion.27
  471.6 69.9 %psum.7 = f32[3584]{0:T(1024)} all-reduce(f32[3584]{0:T(1024)S(1)} %get-tuple-element.9), channel_id=1, replica_groups=mesh['expert'=8,'tensor'=16] {'expert','tensor'}, use_global_device_ids=true, to_apply=%region_10.11 | all-reduce | flops 3584 | bytes 28672 | tf_op jit(solution)/shard_map/psum | solution.py:91
  (32 shorter events, 0.5 us)
Async XLA Ops:
  0.6 61.4 %copy-start = (bf16[128,3584]{1,0:T(8,128)(2,1)S(1)}, bf16[128,3584]{1,0:T(8,128)(2,1)}, u32[]{:S(2)}) copy-start(bf16[128,3584]{1,0:T(8,128)(2,1)} %param.10) | copy-start | bytes 2752516
  0.6 21.1 %copy-start.2 = (bf16[128,3584]{1,0:T(8,128)(2,1)S(1)}, bf16[128,3584]{1,0:T(8,128)(2,1)}, u32[]{:S(2)}) copy-start(bf16[128,3584]{1,0:T(8,128)(2,1)} %param.8) | copy-start | bytes 2752516
  0.7 21.1 %copy-start.5 = (f32[3584]{0:T(1024)S(1)}, f32[3584]{0:T(1024)}, u32[]{:S(2)}) copy-start(f32[3584]{0:T(1024)} %param.9) | copy-start | bytes 43012
  8.9 42.4 %all-to-all-start = ((bf16[128,1,6]{2,1,0:T(2,128)(2,1)}), bf16[128,1,6]{2,1,0:T(2,128)(2,1)S(1)}, u32[]{:S(2)}, u32[]{:S(2)}) async-start(bf16[128,1,6]{2,1,0:T(2,128)(2,1)} %all_to_all.25), calls=%async_computation | async-start | bytes 131072 | tf_op jit(solution)/shard_map/all_to_all | solution.py:67
  51.4 101.3 %all-to-all-start.2 = ((bf16[128,6,3584]{2,1,0:T(8,128)(2,1)}), bf16[128,6,3584]{2,1,0:T(8,128)(2,1)}, u32[]{:S(2)}, u32[]{:S(2)}) async-start(bf16[128,6,3584]{2,1,0:T(8,128)(2,1)} %reshape.173), calls=%async_computation.2 | async-start | bytes 14680064 | tf_op jit(solution)/shard_map/all_to_all | solution.py:65
  152.7 103.4 %all-to-all-start.1 = ((bf16[128,6,3584]{2,1,0:T(8,128)(2,1)}), bf16[128,6,3584]{2,1,0:T(8,128)(2,1)}, u32[]{:S(2)}, u32[]{:S(2)}) async-start(bf16[128,6,3584]{2,1,0:T(8,128)(2,1)} %reshape.171), calls=%async_computation.1 | async-start | bytes 14680064 | tf_op jit(solution)/shard_map/all_to_all | solution.py:66
  176.0 11.9 %copy-start.4 = (bf16[768,3584]{1,0:T(8,128)(2,1)S(1)}, bf16[768,3584]{1,0:T(8,128)(2,1)}, u32[]{:S(2)}) copy-start(bf16[768,3584]{1,0:T(8,128)(2,1)} %reshape.174) | copy-start | bytes 16515076
  279.2 52.5 %all-to-all-start.4 = ((bf16[128,1,6]{2,1,0:T(2,128)(2,1)}), bf16[128,1,6]{2,1,0:T(2,128)(2,1)S(1)}, u32[]{:S(2)}, u32[]{:S(2)}) async-start(bf16[128,1,6]{2,1,0:T(2,128)(2,1)} %convert_element_type.76), calls=%async_computation.4 | async-start | bytes 131072 | tf_op jit(solution)/shard_map/all_to_all | solution.py:83
  292.8 16.2 %copy-start.6 = (f32[768,1024]{1,0:T(8,128)S(1)}, f32[768,1024]{1,0:T(8,128)}, u32[]{:S(2)}) copy-start(f32[768,1024]{1,0:T(8,128)} %fusion.2) | copy-start | bytes 9437188
  292.8 16.2 %copy-start.7 = (f32[768,1024]{1,0:T(8,128)S(1)}, f32[768,1024]{1,0:T(8,128)}, u32[]{:S(2)}) copy-start(f32[768,1024]{1,0:T(8,128)} %get-tuple-element.12) | copy-start | bytes 9437188
  331.7 100.7 %all-to-all-start.3 = ((bf16[128,6,3584]{2,1,0:T(8,128)(2,1)}), bf16[128,6,3584]{2,1,0:T(8,128)(2,1)}, u32[]{:S(2)}, u32[]{:S(2)}) async-start(bf16[128,6,3584]{2,1,0:T(8,128)(2,1)} %reshape.175), calls=%async_computation.3 | async-start | bytes 14680064 | tf_op jit(solution)/shard_map/all_to_all | solution.py:82
  460.8 80.7 %copy-start.1 = (bf16[128,3584]{1,0:T(8,128)(2,1)S(1)}, bf16[128,3584]{1,0:T(8,128)(2,1)}, u32[]{:S(2)}) copy-start(bf16[128,3584]{1,0:T(8,128)(2,1)} %param.10) | copy-start | bytes 2752516
  468.3 1.9 copy-start.3
where the time goes:
time: 549 us; the launch traced here: 542 us
  waiting for transfers between devices  206 us (38%)
  local copies, waits for them, and re-layouts  128 us (23%)
  blocking collectives  69.9 us (13%)
  matrix products  63.1 us (11%)
  starting transfers between devices  59.4 us (11%)
  other arithmetic  14.8 us (3%)
    all_to_all x1, waiting for transfers between devices, shards(): lax.all_to_all(slot_grad, ('expert', 'tensor'), split_axis=0, concat_axis...  85.5 us
    psum x1, blocking collectives, shards(): gain_grad = lax.psum(gain_part, ('expert', 'tensor'))  69.9 us
    all_to_all x1, waiting for transfers between devices, shards(): lax.all_to_all(rows_send, ('expert', 'tensor'), split_axis=0, concat_axis...  61.3 us
    all_to_all x1, waiting for transfers between devices, shards(): lax.all_to_all(grads_send, ('expert', 'tensor'), split_axis=0, concat_axi...  59 us
    scatter x2, local copies, waits for them, and re-layouts, shards(): jnp.zeros((total_rows, model_width), jnp.bfloat16).at[slot_index]  39.5 us
    dot_general x1, matrix products, finish(): lax.dot_general(d_gate, weight_gate, CONTRACT, preferred_element_type=jnp...  16.2 us
    all_to_all x1, starting transfers between devices, shards(): lax.all_to_all(comb_grad, ('expert', 'tensor'), split_axis=0, concat_axis...  13.6 us
    all_to_all x1, starting transfers between devices, shards(): lax.all_to_all(grads_send, ('expert', 'tensor'), split_axis=0, concat_axi...  13.3 us
  transfers between devices with their start and end apart: 5, of which 3 were waited for; matrix products, arithmetic and copies ran while one was open for 25% of the time, Pallas kernels for 0%

commit v1 on v0

v1 whole, which is shorter than its diff:
```python
import jax
import jax.numpy as jnp
from jax import lax
from jax.experimental import pallas as pl
from jax.experimental.pallas import tpu as pltpu
from jax.sharding import PartitionSpec as P

MESH = pl.DeviceIdType.MESH
BF = jnp.bfloat16
F32 = jnp.float32
D = 3584
H = 1024
TOK = 128
CW = 512
NC = D // CW
ROWS = 768
MSG = 48
GTOK = 1024
NT = (((1,), (1,)), ((), ()))
PLANE = ((1, 0), (0, 1), (3, 0), (0, 3), (2, 0), (0, 2), (1, 1), (3, 3), (1, 3), (3, 1), (2, 1), (1, 2), (3, 2), (2, 3), (2, 2))
NS = 3


def device(x, y, z, c):
    return {"expert": (y // 2) * 4 + x, "tensor": z * 4 + (y % 2) * 2 + c}


def mm(a, b):
    return jnp.dot(a, b, preferred_element_type=F32)


def mm_nt(a, b):
    return lax.dot_general(a, b, NT, preferred_element_type=F32)


def kernel(
    hid_ref, gain_ref, ups_ref, rts_ref, cmb_ref, wg_ref, wu_ref, wd_ref,
    out_ref, gout_ref, cout_ref,
    tok, tokaux, gat, gatt, sbuf, saux, rcv, raux, acc_g, acc_u, acc_b,
    wdb, wgb, wub, caux, cret, pbuf, paux, qbuf, qaux, sibaux, ringaux, inv_s, proj_s,
    gall, gring, gsib, gstage,
    w_sem, ag_ss, ag_rr, ag_sr, a_ss, a_rs, a_self, x_ss, x_rs, x_self,
    r_rs, r_self, p_ss, p_rs, q_ss, q_rs, g_ss, g_rs, free_sib, free_ring,
):
    e_i, t_i = lax.axis_index("expert"), lax.axis_index("tensor")
    x, y, z, c = e_i % 4, (e_i // 4) * 2 + (t_i // 2) % 2, t_i // 4, t_i % 2
    me = e_i * 16 + t_i
    plane_me = y * 4 + x
    src_me = c * 4 + z
    sib = device(x, y, z, 1 - c)
    ring = [device(x, y, (z + d) % 4, c) for d in (1, 2, 3)]
    plane = [
        (((y + dy) % 4) * 4 + (x + dx) % 4, device((x + dx) % 4, (y + dy) % 4, z, c)) for dx, dy in PLANE
    ]

    def rows(at, size, align=16):
        return pl.ds(pl.multiple_of(at, align), size)

    def put(src, dst, ss, rs, to):
        pltpu.make_async_remote_copy(
            src_ref=src, dst_ref=dst, send_sem=ss, recv_sem=rs, device_id=to, device_id_type=MESH
        ).start()

    def await_bytes(ref, sem):
        pltpu.make_async_copy(ref, ref, sem).wait()

    def wd_copy(n):
        return pltpu.make_async_copy(
            wd_ref.at[0, :, pl.ds(pl.multiple_of(n * CW, CW), CW)], wdb.at[n % 2], w_sem.at[0, n % 2]
        )

    def wgu_copies(n):
        at = rows(jnp.where(n >= NC, n - NC, n) * CW, CW, CW)
        return (
            pltpu.make_async_copy(wg_ref.at[0, at], wgb.at[n % 2], w_sem.at[1, n % 2]),
            pltpu.make_async_copy(wu_ref.at[0, at], wub.at[n % 2], w_sem.at[2, n % 2]),
        )

    for n in (0, 1):
        wd_copy(n).start()
        for cp in wgu_copies(n):
            cp.start()

    bar = pltpu.get_barrier_semaphore()
    everyone = [sib] + ring + [d for _, d in plane]
    for d in everyone:
        pl.semaphore_signal(bar, inc=1, device_id=d, device_id_type=MESH)

    lane = lax.broadcasted_iota(jnp.int32, (TOK, 128), 1)
    dense = jnp.zeros((TOK, 128), F32)
    for k in range(4):
        wk = cmb_ref[:, k : k + 1].astype(F32) * (1.0 / 65536.0)
        dense = jnp.where(rts_ref[:, k : k + 1] == lane, wk, dense)
    own = rows(src_me * TOK, TOK, TOK)
    tokaux[own, :] = dense.astype(BF)
    for k in range(NC):
        tok[k, own, :] = ups_ref[:, k * CW : (k + 1) * CW]

    pl.semaphore_wait(bar, len(everyone))

    def ag_send(k):
        for d in [*ring, sib]:
            rs = ag_sr.at[k] if d is sib else ag_rr.at[k]
            put(tok.at[k, own], tok.at[k, own], ag_ss.at[k], rs, d)

    def ag_forward(k):
        await_bytes(tok.at[k, pl.ds(0, 3 * TOK)], ag_rr.at[k])
        for d in (1, 2, 3):
            at = rows((c * 4 + (z + d) % 4) * TOK, TOK, TOK)
            put(tok.at[k, at], tok.at[k, at], ag_ss.at[k], ag_sr.at[k], sib)

    def ag_await(k):
        await_bytes(tok.at[k, pl.ds(0, 4 * TOK)], ag_sr.at[k])
        await_bytes(tok.at[k, pl.ds(0, 7 * TOK)], ag_ss.at[k])

    for d in [*ring, sib]:
        put(tokaux.at[own], tokaux.at[own], x_ss.at[0], x_rs.at[1 if d is sib else 0], d)
    ag_send(0)
    ag_send(1)

    total = jnp.zeros((TOK, CW), F32)
    for k in range(NC):
        h = hid_ref[:, k * CW : (k + 1) * CW].astype(F32)
        total = total + h * h
    inv = lax.rsqrt(jnp.sum(total, axis=1, keepdims=True) * (1.0 / D) + 1e-06)
    inv_s[...] = jnp.broadcast_to(inv, (TOK, 128))
    for k in range(NC):
        cols = slice(k * CW, (k + 1) * CW)
        unit = hid_ref[:, cols].astype(F32) * inv
        tok[NC + k, own, :] = (unit * gain_ref[:, cols]).astype(BF)

    await_bytes(tokaux.at[pl.ds(0, 3 * TOK)], x_rs.at[0])
    for d in (1, 2, 3):
        at = rows((c * 4 + (z + d) % 4) * TOK, TOK, TOK)
        put(tokaux.at[at], tokaux.at[at], x_ss.at[0], x_rs.at[1], sib)
    await_bytes(tokaux.at[pl.ds(0, 4 * TOK)], x_rs.at[1])
    await_bytes(tokaux.at[pl.ds(0, 7 * TOK)], x_ss.at[0])

    slot = lax.broadcasted_iota(jnp.int32, (8, ROWS), 1)
    peer = jnp.zeros((8, ROWS), jnp.int32)
    for m in range(1, 16):
        peer = peer + (slot >= MSG * m).astype(jnp.int32)
    rest = slot - MSG * peer
    source = jnp.zeros((8, ROWS), jnp.int32)
    for m in range(1, 8):
        source = source + (rest >= 6 * m).astype(jnp.int32)
    place = (rest - 6 * source + 1).astype(F32)
    py = lax.shift_right_logical(peer, 2)
    px = lax.bitwise_and(peer, 3)
    peer_expert = (
        (lax.shift_right_logical(py, 1) * 4 + px) * 16 + z * 4 + lax.bitwise_and(py, 1) * 2 + c
    )
    pick = (
        lax.broadcasted_iota(jnp.int32, (128, ROWS), 0) == jnp.broadcast_to(peer_expert[0:1], (128, ROWS))
    ).astype(F32).astype(BF)
    below = (
        lax.broadcasted_iota(jnp.int32, (TOK, TOK), 0) > lax.broadcasted_iota(jnp.int32, (TOK, TOK), 1)
    ).astype(F32).astype(BF)
    for s in range(8):
        named = (tokaux[s * TOK : (s + 1) * TOK, :].astype(F32) != 0.0).astype(F32)
        code = (mm(below, named.astype(BF)) + 1.0) * named
        want = jnp.where(source[0:1] == s, place[0:1], -1.0)
        hot = (mm(code.astype(BF), pick) == jnp.broadcast_to(want, (TOK, ROWS))).astype(F32)
        gatt[s * TOK : (s + 1) * TOK, :] = hot.astype(BF)
        gat[:, s * TOK : (s + 1) * TOK] = jnp.transpose(hot).astype(BF)

    saux[...] = mm(gat[...], tokaux[...]).astype(BF)
    mine = rows(plane_me * MSG, MSG)
    for p, d in plane:
        put(saux.at[rows(p * MSG, MSG)], raux.at[mine], x_ss.at[1], x_rs.at[2], d)
    pltpu.make_async_copy(saux.at[mine], raux.at[mine], x_self.at[0]).start()

    def spread(buf, dst, rs, self_sem):
        for p, d in plane:
            put(sbuf.at[buf, rows(p * MSG, MSG)], dst.at[mine], a_ss.at[buf], rs, d)
        pltpu.make_async_copy(sbuf.at[buf, mine], dst.at[mine], self_sem).start()

    def await_spread(dst, rs, self_sem):
        await_bytes(dst.at[pl.ds(0, 15 * MSG)], rs)
        await_bytes(dst.at[pl.ds(0, MSG)], self_sem)

    def await_sbuf(buf):
        await_bytes(sbuf.at[buf, pl.ds(0, 15 * MSG)], a_ss.at[buf])

    ag_forward(0)
    RB = 256

    def dispatch(i, carry):
        @pl.when(i < 2 * NC)
        def _():
            buf = lax.rem(i, NS)
            ag_await(i)

            @pl.when(i >= NS)
            def _():
                await_sbuf(buf)

            def gather(r, cc):
                at = rows(r * RB, RB, RB)
                sbuf[buf, at, :] = mm(gat[at, :], tok[i]).astype(BF)
                return cc

            lax.fori_loop(0, ROWS // RB, gather, 0)
            spread(buf, rcv.at[i], a_rs.at[i], a_self.at[i])

        @pl.when(i + 2 < 2 * NC)
        def _():
            ag_send(i + 2)

        @pl.when(i + 1 < 2 * NC)
        def _():
            ag_forward(i + 1)

        @pl.when(i >= 2)
        def _():
            j = i - 2
            await_spread(rcv.at[j], a_rs.at[j], a_self.at[j])

            @pl.when(j < NC)
            def _():
                wd_copy(j).wait()

                def step(r, cc):
                    at = rows(r * RB, RB, RB)
                    got = mm_nt(rcv[j, at, :], wdb[lax.rem(j, 2)])

                    @pl.when(j == 0)
                    def _():
                        acc_b[at, :] = got

                    @pl.when(j > 0)
                    def _():
                        acc_b[at, :] += got

                    return cc

                lax.fori_loop(0, ROWS // RB, step, 0)

                @pl.when(j + 2 < NC)
                def _():
                    wd_copy(j + 2).start()

            @pl.when(j >= NC)
            def _():
                n = j - NC
                for cp in wgu_copies(n):
                    cp.wait()

                def step(r, cc):
                    at = rows(r * RB, RB, RB)
                    for acc, w in ((acc_g, wgb), (acc_u, wub)):
                        got = mm(rcv[j, at, :], w[lax.rem(n, 2)])

                        @pl.when(n == 0)
                        def _():
                            acc[at, :] = got

                        @pl.when(n > 0)
                        def _():
                            acc[at, :] += got

                    return cc

                lax.fori_loop(0, ROWS // RB, step, 0)
                for cp in wgu_copies(n + 2):
                    cp.start()

        return carry

    lax.fori_loop(0, 2 * NC + 2, dispatch, 0)

    pl.semaphore_signal(free_sib, inc=1, device_id=sib, device_id_type=MESH)
    for d in ring:
        pl.semaphore_signal(free_ring, inc=1, device_id=d, device_id_type=MESH)

    await_bytes(raux.at[pl.ds(0, 15 * MSG)], x_rs.at[2])
    await_bytes(raux.at[pl.ds(0, MSG)], x_self.at[0])
    await_bytes(saux.at[pl.ds(0, 15 * MSG)], x_ss.at[1])
    AB = 64
    alane = lax.broadcasted_iota(jnp.int32, (AB, 128), 1)

    def activate(r, cc):
        at = rows(r * AB, AB, AB)
        scale = jnp.sum(jnp.where(alane == me, raux[at, :].astype(F32), 0.0), axis=1, keepdims=True)
        comb = jnp.zeros((AB, 1), F32)
        for half in range(2):
            cols = slice(half * CW, (half + 1) * CW)
            gate, up, back = acc_g[at, cols], acc_u[at, cols], acc_b[at, cols]
            sig = jax.nn.sigmoid(gate)
            act = gate * sig
            comb = comb + jnp.sum(act * up * back, axis=1, keepdims=True)
            scaled = scale * back
            rcv[half, at, :] = (scaled * up * sig * (1.0 + gate * (1.0 - sig))).astype(BF)
            rcv[2 + half, at, :] = (scaled * act).astype(BF)
        caux[at, :] = jnp.where(alane == me, comb, 0.0).astype(BF)
        return cc

    lax.fori_loop(0, ROWS // AB, activate, 0)

    for p, d in plane:
        put(caux.at[rows(p * MSG, MSG)], cret.at[mine], x_ss.at[2], x_rs.at[3], d)
    pltpu.make_async_copy(caux.at[mine], cret.at[mine], x_self.at[1]).start()

    half_me, half_sib = rows(c * 512, 512, 512), rows((1 - c) * 512, 512, 512)

    def own_part(k):
        return pl.ds(0, 512), pl.ds(pl.multiple_of(lax.rem(k, 2) * CW, CW), CW)

    def grad_part(k):
        return rows(lax.div(k, 2) * TOK, TOK, TOK), pl.ds(pl.multiple_of(lax.rem(k, 2) * CW, CW), CW)

    def send_back(i):
        n = i + NC
        buf = lax.rem(i + 2 * NC, NS)
        await_sbuf(buf)
        for cp in wgu_copies(n):
            cp.wait()

        def step(r, gsum):
            at = rows(r * RB, RB, RB)
            got = mm_nt(rcv[0, at, :], wgb[lax.rem(n, 2), :, 0:CW])
            got = got + mm_nt(rcv[1, at, :], wgb[lax.rem(n, 2), :, CW:H])
            got = got + mm_nt(rcv[2, at, :], wub[lax.rem(n, 2), :, 0:CW])
            got = got + mm_nt(rcv[3, at, :], wub[lax.rem(n, 2), :, CW:H])
            cut = got.astype(BF)
            sbuf[buf, at, :] = cut
            prod = cut.astype(F32) * rcv[NC + i, at, :].astype(F32)
            return gsum + jnp.sum(prod, axis=0, keepdims=True)

        gsum = lax.fori_loop(0, ROWS // RB, step, jnp.zeros((1, CW), F32))
        gstage[:, pl.ds(pl.multiple_of(i * CW, CW), CW)] = gsum
        spread(buf, tok.at[i], r_rs.at[i], r_self.at[i])

        @pl.when(i + 2 < NC)
        def _():
            for cp in wgu_copies(n + 2):
                cp.start()

    def combine(k):
        b = lax.rem(k, 2)
        await_spread(tok.at[k], r_rs.at[k], r_self.at[k])

        @pl.when(k >= 2)
        def _():
            await_bytes(pbuf.at[b], p_ss.at[b])

        ret = tok.at[k]
        pbuf[b] = mm(gatt[half_sib, :], ret[0:ROWS, :]).astype(BF)
        put(pbuf.at[b], tok.at[NC + k, pl.ds(0, 512)], p_ss.at[b], p_rs.at[k], sib)
        at, cols = own_part(k)
        acc_g[at, cols] = mm(gatt[half_me, :], ret[0:ROWS, :])

    def scatter(k):
        b = lax.rem(k, 2)
        await_bytes(tok.at[NC + k, pl.ds(0, 512)], p_rs.at[k])

        @pl.when(k >= 2)
        def _():
            await_bytes(qbuf.at[b], q_ss.at[b])

        _, cols = own_part(k)
        for d in (1, 2, 3):
            at = rows(((z + d) % 4) * TOK, TOK, TOK)
            qbuf[b, (d - 1) * TOK : d * TOK, :] = (acc_g[at, cols] + tok[NC + k, at, :].astype(F32)).astype(BF)
            put(
                qbuf.at[b, pl.ds((d - 1) * TOK, TOK)], tok.at[NC + k, pl.ds(512 + (d - 1) * TOK, TOK)],
                q_ss.at[b], q_rs.at[k], ring[d - 1],
            )
        at = rows(z * TOK, TOK, TOK)
        grow, gcol = grad_part(k)
        acc_u[grow, gcol] = acc_g[at, cols] + tok[NC + k, at, :].astype(F32)

    def settle(k):
        await_bytes(tok.at[NC + k, pl.ds(512, 384)], q_rs.at[k])
        grow, gcol = grad_part(k)
        grad = acc_u[grow, gcol]
        for d in range(3):
            grad = grad + tok[NC + k, 512 + d * TOK : 512 + (d + 1) * TOK, :].astype(F32)
        cols = pl.ds(pl.multiple_of(k * CW, CW), CW)
        scaled = grad * gain_ref[:, cols]
        acc_u[grow, gcol] = scaled
        proj_s[...] += scaled * (hid_ref[:, cols].astype(F32) * inv_s[:, 0:1])

    proj_s[...] = jnp.zeros_like(proj_s)

    def back(i, carry):
        @pl.when(i < NC)
        def _():
            send_back(i)

        @pl.when(i == 2)
        def _():
            pl.semaphore_wait(free_sib, 1)
            pl.semaphore_wait(free_ring, 3)

        @pl.when(i == 3)
        def _():
            await_bytes(cret.at[pl.ds(0, 15 * MSG)], x_rs.at[3])
            await_bytes(cret.at[pl.ds(0, MSG)], x_self.at[1])
            await_bytes(caux.at[pl.ds(0, 15 * MSG)], x_ss.at[2])
            paux[...] = mm(gatt[half_sib, :], cret[...]).astype(BF)
            put(paux, sibaux, x_ss.at[3], x_rs.at[4], sib)

        @pl.when(i == 5)
        def _():
            await_bytes(sibaux, x_rs.at[4])
            await_bytes(paux, x_ss.at[3])
            qaux[...] = (mm(gatt[half_me, :], cret[...]) + sibaux[...].astype(F32)).astype(BF)
            for d in (1, 2, 3):
                at = rows(((z + d) % 4) * TOK, TOK, TOK)
                put(qaux.at[at], ringaux.at[pl.ds((d - 1) * TOK, TOK)], x_ss.at[4], x_rs.at[5], ring[d - 1])

        @pl.when(i == NC - 1)
        def _():
            gall[plane_me] = gstage[...]
            for _, d in plane:
                put(gall.at[plane_me], gall.at[plane_me], g_ss.at[0], g_rs.at[0], d)

        @pl.when(jnp.logical_and(i >= 2, i < NC + 2))
        def _():
            combine(i - 2)

        @pl.when(jnp.logical_and(i >= 3, i < NC + 3))
        def _():
            scatter(i - 3)

        @pl.when(i == NC)
        def _():
            await_bytes(gall.at[pl.ds(0, 15)], g_rs.at[0])
            await_bytes(gall.at[pl.ds(0, 15)], g_ss.at[0])
            gring[z] = jnp.sum(gall[...], axis=0)
            for d in ring:
                put(gring.at[z], gring.at[z], g_ss.at[1], g_rs.at[1], d)

        @pl.when(i == NC + 1)
        def _():
            await_bytes(gring.at[pl.ds(0, 3)], g_rs.at[1])
            await_bytes(gring.at[pl.ds(0, 3)], g_ss.at[1])
            gsib[c] = gring[0] + gring[1] + gring[2] + gring[3]
            put(gsib.at[c], gsib.at[c], g_ss.at[2], g_rs.at[2], sib)

        @pl.when(i >= 4)
        def _():
            settle(i - 4)

        return carry

    lax.fori_loop(0, NC + 4, back, 0)

    project = jnp.sum(proj_s[...], axis=1, keepdims=True) * (1.0 / D)
    inv = inv_s[:, 0:1]
    for k in range(NC):
        cols = slice(k * CW, (k + 1) * CW)
        scaled = acc_u[(k // 2) * TOK : (k // 2 + 1) * TOK, (k % 2) * CW : (k % 2 + 1) * CW]
        unit = hid_ref[:, cols].astype(F32) * inv
        out_ref[:, cols] = (inv * (scaled - unit * project)).astype(BF)

    await_bytes(gsib.at[pl.ds(0, 1)], g_rs.at[2])
    await_bytes(gsib.at[pl.ds(0, 1)], g_ss.at[2])
    gout_ref[...] = (gsib[0] + gsib[1]) / gain_ref[...]

    await_bytes(ringaux, x_rs.at[5])
    await_bytes(ringaux, x_ss.at[4])
    mine_q = rows(z * TOK, TOK, TOK)
    cfin = qaux[mine_q, :].astype(F32)
    for d in range(3):
        cfin = cfin + ringaux[d * TOK : (d + 1) * TOK, :].astype(F32)
    for k in range(4):
        got = jnp.sum(jnp.where(rts_ref[:, k : k + 1] == lane, cfin, 0.0), axis=1, keepdims=True)
        cout_ref[:, k : k + 1] = got.astype(BF)

    for b in range(NS):
        await_sbuf(b)
    for b in range(2):
        await_bytes(pbuf.at[b], p_ss.at[b])
        await_bytes(qbuf.at[b], q_ss.at[b])


def shards(hidden_in, norm_gain, upstream, routes, combine_fixed, w_gate, w_up, w_down):
    vm = pl.BlockSpec(memory_space=pltpu.VMEM)
    hbm = pl.BlockSpec(memory_space=pl.ANY)
    dma = pltpu.SemaphoreType.DMA
    out, gain_grad, combine_grad = pl.pallas_call(
        kernel,
        out_shape=(
            jax.ShapeDtypeStruct((TOK, D), BF),
            jax.ShapeDtypeStruct((1, D), F32),
            jax.ShapeDtypeStruct((TOK, 4), BF),
        ),
        in_specs=[vm, vm, vm, vm, vm, hbm, hbm, hbm],
        out_specs=(vm, vm, vm),
        scratch_shapes=[
            pltpu.VMEM((2 * NC, GTOK, CW), BF),
            pltpu.VMEM((GTOK, 128), BF),
            pltpu.VMEM((ROWS, GTOK), BF),
            pltpu.VMEM((GTOK, ROWS), BF),
            pltpu.VMEM((NS, ROWS, CW), BF),
            pltpu.VMEM((ROWS, 128), BF),
            pltpu.VMEM((2 * NC, ROWS, CW), BF),
            pltpu.VMEM((ROWS, 128), BF),
            pltpu.VMEM((ROWS, H), F32),
            pltpu.VMEM((ROWS, H), F32),
            pltpu.VMEM((ROWS, H), F32),
            pltpu.VMEM((2, H, CW), BF),
            pltpu.VMEM((2, CW, H), BF),
            pltpu.VMEM((2, CW, H), BF),
            pltpu.VMEM((ROWS, 128), BF),
            pltpu.VMEM((ROWS, 128), BF),
            pltpu.VMEM((2, 512, CW), BF),
            pltpu.VMEM((512, 128), BF),
            pltpu.VMEM((2, 384, CW), BF),
            pltpu.VMEM((512, 128), BF),
            pltpu.VMEM((512, 128), BF),
            pltpu.VMEM((384, 128), BF),
            pltpu.VMEM((TOK, 128), F32),
            pltpu.VMEM((TOK, CW), F32),
            pltpu.VMEM((16, 1, D), F32),
            pltpu.VMEM((4, 1, D), F32),
            pltpu.VMEM((2, 1, D), F32),
            pltpu.VMEM((1, D), F32),
            dma((3, 2)),
            dma((2 * NC,)),
            dma((2 * NC,)),
            dma((2 * NC,)),
            dma((NS,)),
            dma((2 * NC,)),
            dma((2 * NC,)),
            dma((5,)),
            dma((6,)),
            dma((2,)),
            dma((NC,)),
            dma((NC,)),
            dma((2,)),
            dma((NC,)),
            dma((2,)),
            dma((NC,)),
            dma((3,)),
            dma((3,)),
            pltpu.SemaphoreType.REGULAR,
            pltpu.SemaphoreType.REGULAR,
        ],
        compiler_params=pltpu.CompilerParams(
            collective_id=0, has_side_effects=True, vmem_limit_bytes=62 * 2**20
        ),
        cost_estimate=pl.CostEstimate(flops=50 * 10**9, bytes_accessed=40 * 10**6, transcendentals=10**6),
    )(hidden_in, norm_gain[None, :], upstream, routes, combine_fixed, w_gate, w_up, w_down)
    return out, gain_grad.reshape(D), combine_grad


def solution(mesh):
    split = ("expert", "tensor")
    in_specs = (
        P(split, None),
        P(),
        P(split, None),
        P(split, None),
        P(split, None),
        P(split, None, None),
        P(split, None, None),
        P(split, None, None),
    )
    out_specs = (P(split, None), P(), P(split, None))
    return jax.shard_map(shards, mesh=mesh, in_specs=in_specs, out_specs=out_specs, check_vma=False)
```

time: 549 us -> 247 us (0.45); the launches traced: 542 us -> 246 us
  Pallas kernels: 0 us -> 237 us
  waiting for transfers between devices: 206 us -> 0 us
  local copies, waits for them, and re-layouts: 128 us -> 7.71 us
  blocking collectives: 69.9 us -> 0 us
  matrix products: 63.1 us -> 0 us
  starting transfers between devices: 59.4 us -> 0 us
  other arithmetic: 14.8 us -> 1.35 us
    pallas_call x0 -> x1, Pallas kernels: none -> 237 us  [shards(): pl.pallas_call(kernel, out_shape=(jax.ShapeDtypeStruct((TOK, D), BF), jax...]
    all_to_all x5 -> x0, waiting for transfers between devices: 206 us -> none  [the longest x1 85.5 us: shards(): lax.all_to_all(slot_grad, ('expert', 'tensor'), split_axis=0, concat_axis...]
    psum x1 -> x0, blocking collectives: 69.9 us -> none  [shards(): gain_grad = lax.psum(gain_part, ('expert', 'tensor'))]
    dot_general x5 -> x0, matrix products: 63.1 us -> none  [the longest x1 16.2 us: finish(): lax.dot_general(d_gate, weight_gate, CONTRACT, preferred_element_type=jnp...]
    all_to_all x5 -> x0, starting transfers between devices: 59.4 us -> none  [the longest x1 13.6 us: shards(): lax.all_to_all(comb_grad, ('expert', 'tensor'), split_axis=0, concat_axis...]
    reshape x9 -> x0, local copies, waits for them, and re-layouts: 58.1 us -> none  [the longest x1 9.69 us: shards(): rows_recv.reshape(total_rows, model_width)]
    scatter x3 -> x0, local copies, waits for them, and re-layouts: 43.3 us -> none  [the longest x2 39.5 us: shards(): jnp.zeros((total_rows, model_width), jnp.bfloat16).at[slot_index]]
    gather x2 -> x0, local copies, waits for them, and re-layouts: 14.7 us -> none  [the longest x1 11.2 us: shards(): picked = slot_back[slot_index].reshape(tok_rows, top_count, model_width)]
  transfers between devices with their start and end apart: 5 -> 0, of which waited for: 3 -> 0; matrix products, arithmetic and copies ran while one was open for 25% -> 0% of each run, Pallas kernels for 0% -> 0%
where the time goes in v1:
time: 247 us; the launch traced here: 246 us
  Pallas kernels  237 us (96%)
  local copies, waits for them, and re-layouts  7.71 us (3%)
    pallas_call x1, Pallas kernels, shards(): pl.pallas_call(kernel, out_shape=(jax.ShapeDtypeStruct((TOK, D), BF), jax...  237 us
    unnamed x4, local copies, waits for them, and re-layouts  6.38 us

profile of v1, /device:TPU:0, one launch (start us, length us, event | category | flops | bytes accessed | tf_op | source)
XLA Modules:
  0.0 246.3 jit_solution(16631215696470322690)
XLA Ops:
  0.6 1.3 broadcast_in_dim.3.gain_ref
  2.0 1.4 copy.11.rts_ref
  3.4 1.4 copy.12.cmb_ref
  4.8 236.6 %shard_map.103 = (bf16[128,3584]{1,0:T(8,128)(2,1)}, f32[1,3584]{1,0:T(1,128)}, bf16[128,4]{1,0:T(8,128)(2,1)}) custom-call(bf16[128,3584]{1,0:T(8,128)(2,1)} %hid_ref.1, f32[1,3584]{1,0:T(1,128)} %broadcast_in_dim.3.gain_ref, bf16[128,3584]{1,0:T(8,128)(2,1)} %ups_ref.1, s32[128,4]{1,0:T(8,128)} %copy.11.rts_ref, s32[128,4]{1,0:T(8,128)} %copy.12.cmb_ref, ...), custom_call_target="tpu_custom_call" | custom-call | flops 49999998976 | bytes 40000000 | tf_op jit(solution)/shard_map/pallas_call | solution.py:483
  241.4 1.4 copy.13
  242.8 1.4 reduce
  244.1 2.2 copy.15

commit v2 on v1

v2 whole, which is shorter than its diff:
```python
import jax
import jax.numpy as jnp
from jax import lax
from jax.experimental import pallas as pl
from jax.experimental.pallas import tpu as pltpu
from jax.sharding import PartitionSpec as P

MESH = pl.DeviceIdType.MESH
BF = jnp.bfloat16
F32 = jnp.float32
D = 3584
H = 1024
TOK = 128
CW = 512
NC = D // CW
ROWS = 768
MSG = 48
GTOK = 1024
HALF = TOK // 2
NT = (((1,), (1,)), ((), ()))
PLANE = ((1, 0), (0, 1), (3, 0), (0, 3), (2, 0), (0, 2), (1, 1), (3, 3), (1, 3), (3, 1), (2, 1), (1, 2), (3, 2), (2, 3), (2, 2))
NS = 4
RB = 256
AB = 64
L1, L2, L3 = 7, 5, 3
K1, K2, K3, K4 = 2, 4, 5, 7
LAG = 3


def device(x, y, z, c):
    return {"expert": (y // 2) * 4 + x, "tensor": z * 4 + (y % 2) * 2 + c}


def mm(a, b):
    return jnp.dot(a, b, preferred_element_type=F32)


def mm_nt(a, b):
    return lax.dot_general(a, b, NT, preferred_element_type=F32)


def rows(at, size, align=16):
    return pl.ds(pl.multiple_of(at, align), size)


class Frame:
    def __init__(self, a, x, y, z, c):
        self.is0 = (a - 1) * (a - 2) // 2
        self.is1 = a * (2 - a)
        self.is2 = a * (a - 1) // 2
        self.u = (1 - self.is1) * y + self.is1 * z
        self.v = (1 - self.is0) * x + self.is0 * z
        self.r = self.is2 * z + self.is0 * x + self.is1 * y
        self.c = c

    def coords(self, u, v, r):
        return (
            self.is0 * r + (1 - self.is0) * v,
            self.is1 * r + (1 - self.is1) * u,
            self.is2 * r + self.is0 * v + self.is1 * u,
        )

    def ring(self, d):
        return device(*self.coords(self.u, self.v, (self.r + d) % 4), self.c)

    def peers(self):
        for dv, du in PLANE:
            u, v = (self.u + du) % 4, (self.v + dv) % 4
            yield u * 4 + v, device(*self.coords(u, v, self.r), self.c)

    def place(self):
        return self.u * 4 + self.v


def kernel(
    hid_ref, gain_ref, ups_ref, rts_ref, cmb_ref, wg_ref, wu_ref, wd_ref,
    out_ref, gout_ref, cout_ref,
    tok, tokaux, gat, gatt, perm, sbuf, saux, rcv, raux, canon, acc, hid, gain, turn,
    wdb, wgb, wub, caux, cret, pbuf, paux, q1buf, q2buf, qaux, sibaux, ringaux, inv_s, proj_s,
    gall, gring, gsib, gstage,
    i_sem, w_sem, ag_ss, ag_r1, ag_r2, ag_sr, aux_r, aux_s, aux_ss, a_ss, a_rs, a_self, x_ss, x_rs, x_self,
    r_rs, r_self, p_ss, p_rs, q1_ss, q1_rs, q2_ss, q2_rs, g_ss, g_rs, free_sib, free_ring,
):
    e_i, t_i = lax.axis_index("expert"), lax.axis_index("tensor")
    x, y, z, c = e_i % 4, (e_i // 4) * 2 + (t_i // 2) % 2, t_i // 4, t_i % 2
    me = e_i * 16 + t_i
    sib = device(x, y, z, 1 - c)

    def frame(a):
        return Frame(a, x, y, z, c)

    def axis(i):
        return lax.rem(i + 1, 3)

    def back_axis(k):
        return lax.rem(k + 2, 3)

    def own(f):
        return rows((c * 4 + f.r) * TOK, TOK, TOK)

    def ring_rows(f, d):
        return rows((c * 4 + (f.r + d) % 4) * TOK, TOK, TOK)

    def put(src, dst, ss, rs, to):
        pltpu.make_async_remote_copy(
            src_ref=src, dst_ref=dst, send_sem=ss, recv_sem=rs, device_id=to, device_id_type=MESH
        ).start()

    def await_bytes(ref, sem):
        pltpu.make_async_copy(ref, ref, sem).wait()

    def await_once(ref, sem, n):
        await_bytes(ref.at[pl.ds(0, n)], sem)

    zf = frame(2)
    bar = pltpu.get_barrier_semaphore()
    everyone = [sib]
    for dx in range(4):
        for dy in range(4):
            for dz in range(4):
                if 0 in (dx, dy, dz) and (dx or dy or dz):
                    everyone.append(device((x + dx) % 4, (y + dy) % 4, (z + dz) % 4, c))
    for d in everyone:
        pl.semaphore_signal(bar, inc=1, device_id=d, device_id_type=MESH)

    for k in range(NC):
        pltpu.make_async_copy(
            ups_ref.at[:, pl.ds(k * CW, CW)], tok.at[k, own(frame((k + 1) % 3))], i_sem.at[0]
        ).start()
    pltpu.make_async_copy(hid_ref, hid, i_sem.at[1]).start()

    def wd_copy(n):
        return pltpu.make_async_copy(
            wd_ref.at[0, :, pl.ds(pl.multiple_of(n * CW, CW), CW)], wdb.at[n % 2], w_sem.at[0, n % 2]
        )

    def wgu_copies(n):
        at = rows(jnp.where(n >= NC, n - NC, n) * CW, CW, CW)
        return (
            pltpu.make_async_copy(wg_ref.at[0, at], wgb.at[n % 2], w_sem.at[1, n % 2]),
            pltpu.make_async_copy(wu_ref.at[0, at], wub.at[n % 2], w_sem.at[2, n % 2]),
        )

    for n in (0, 1):
        wd_copy(n).start()
        for cp in wgu_copies(n):
            cp.start()

    lane = lax.broadcasted_iota(jnp.int32, (TOK, 128), 1)
    turn[0:4, :] = rts_ref[...].astype(F32)
    turn[4:8, :] = cmb_ref[...].astype(F32) * (1.0 / 65536.0)
    turned = jnp.transpose(turn[...])
    lane_f = lane.astype(F32)
    dense = jnp.zeros((TOK, 128), F32)
    for k in range(4):
        dense = jnp.where(turned[:, k : k + 1] == lane_f, turned[:, 4 + k : 5 + k], dense)
    dense = dense.astype(BF)
    for a in range(3):
        tokaux[a, own(frame(a)), :] = dense
    for r in range(D // 128):
        gain[:, r * 128 : (r + 1) * 128] = gain_ref[r : r + 1, :]

    pl.semaphore_wait(bar, len(everyone))

    for a in (1, 2, 0):
        f = frame(a)
        at = own(f)
        for d in (1, 3, 2):
            put(tokaux.at[a, at], tokaux.at[a, at], aux_ss.at[a], aux_r.at[a], f.ring(d))
        put(tokaux.at[a, at], tokaux.at[a, at], aux_ss.at[a], aux_s.at[a], sib)

    def ag_first(i):
        f = frame(axis(i))
        at = own(f)
        put(tok.at[i, at], tok.at[i, at], ag_ss.at[i], ag_r1.at[i], f.ring(1))
        put(tok.at[i, at], tok.at[i, at], ag_ss.at[i], ag_r1.at[i], f.ring(3))
        put(tok.at[i, at], tok.at[i, at], ag_ss.at[i], ag_sr.at[i], sib)

    def ag_second(i):
        f = frame(axis(i))
        await_once(tok.at[i], ag_r1.at[i], 2 * TOK)
        for d, part in ((3, 0), (1, HALF)):
            at = rows((c * 4 + (f.r + d) % 4) * TOK + part, HALF, HALF)
            put(tok.at[i, at], tok.at[i, at], ag_ss.at[i], ag_r2.at[i], f.ring(4 - d))
        for d in (3, 1):
            at = ring_rows(f, d)
            put(tok.at[i, at], tok.at[i, at], ag_ss.at[i], ag_sr.at[i], sib)

    def ag_third(i):
        f = frame(axis(i))
        await_once(tok.at[i], ag_r2.at[i], TOK)
        at = ring_rows(f, 2)
        put(tok.at[i, at], tok.at[i, at], ag_ss.at[i], ag_sr.at[i], sib)

    await_once(tok.at[0], i_sem.at[0], 7 * TOK)
    for i in range(3):
        ag_first(i)

    slot = lax.broadcasted_iota(jnp.int32, (8, ROWS), 1)
    peer = jnp.zeros((8, ROWS), jnp.int32)
    for m in range(1, 16):
        peer = peer + (slot >= MSG * m).astype(jnp.int32)
    rest = slot - MSG * peer
    source = jnp.zeros((8, ROWS), jnp.int32)
    for m in range(1, 8):
        source = source + (rest >= 6 * m).astype(jnp.int32)
    place = rest - 6 * source
    pu, pv = lax.shift_right_logical(peer, 2), lax.bitwise_and(peer, 3)
    sc, sr = lax.shift_right_logical(source, 2), lax.bitwise_and(source, 3)

    def build(a):
        f = frame(a)
        await_once(tokaux.at[a], aux_s.at[a], 4 * TOK)
        await_once(tokaux.at[a], aux_ss.at[a], 7 * TOK)
        px, py, pz = f.coords(pu, pv, jnp.zeros_like(pu) + f.r)
        expert = (
            (lax.shift_right_logical(py, 1) * 4 + px) * 16 + pz * 4 + lax.bitwise_and(py, 1) * 2 + c
        )
        pick = (
            lax.broadcasted_iota(jnp.int32, (128, ROWS), 0) == jnp.broadcast_to(expert[0:1], (128, ROWS))
        ).astype(F32).astype(BF)
        below = (
            lax.broadcasted_iota(jnp.int32, (TOK, TOK), 0) > lax.broadcasted_iota(jnp.int32, (TOK, TOK), 1)
        ).astype(F32).astype(BF)
        for s in range(8):
            part = slice(s * TOK, (s + 1) * TOK)
            named = (tokaux[a, part, :].astype(F32) != 0.0).astype(F32)
            code = (mm(below, named.astype(BF)) + 1.0) * named
            want = jnp.where(source[0:1] == s, (place[0:1] + 1).astype(F32), -1.0)
            hot = (mm(code.astype(BF), pick) == jnp.broadcast_to(want, (TOK, ROWS))).astype(F32)
            gatt[a, part, :] = hot.astype(BF)
            gat[a, :, part] = jnp.transpose(hot).astype(BF)

    def swaps():
        swap_x = (pu * 4 + sr) * MSG + (sc * 4 + pv) * 6 + place
        swap_y = (sr * 4 + pv) * MSG + (sc * 4 + pu) * 6 + place
        at = lax.broadcasted_iota(jnp.int32, (ROWS, ROWS), 0)
        for a, to in ((0, swap_x), (1, swap_y)):
            perm[a] = (at == jnp.broadcast_to(to[0:1], (ROWS, ROWS))).astype(F32).astype(BF)

    def norm():
        await_bytes(hid, i_sem.at[1])
        total = jnp.zeros((TOK, CW), F32)
        for k in range(NC):
            h = hid[:, k * CW : (k + 1) * CW].astype(F32)
            total = total + h * h
        inv = lax.rsqrt(jnp.sum(total, axis=1, keepdims=True) * (1.0 / D) + 1e-06)
        inv_s[...] = jnp.broadcast_to(inv, (TOK, 128))
        for k in range(NC):
            cols = slice(k * CW, (k + 1) * CW)
            unit = hid[:, cols].astype(F32) * inv
            tok[NC + k, own(frame((NC + k + 1) % 3)), :] = (unit * gain[:, cols]).astype(BF)

    norm()
    for a in (1, 2, 0):
        f = frame(a)
        await_once(tokaux.at[a], aux_r.at[a], 3 * TOK)
        for d in (1, 3, 2):
            at = ring_rows(f, d)
            put(tokaux.at[a, at], tokaux.at[a, at], aux_ss.at[a], aux_s.at[a], sib)
    for i in range(3):
        ag_second(i)
    for i in range(3, 6):
        ag_first(i)
    build(1)
    for i in range(3):
        ag_third(i)
    swaps()
    ag_second(3)

    def spread(f, buf, dst, rs, self_sem):
        mine = rows(f.place() * MSG, MSG)
        for p, d in f.peers():
            put(sbuf.at[buf, rows(p * MSG, MSG)], dst.at[mine], a_ss.at[buf], rs, d)
        pltpu.make_async_copy(sbuf.at[buf, mine], dst.at[mine], self_sem).start()

    def await_spread(dst, rs, self_sem):
        await_once(dst, rs, 15 * MSG)
        await_once(dst, self_sem, MSG)

    def await_sbuf(buf):
        await_once(sbuf.at[buf], a_ss.at[buf], 15 * MSG)

    def by_rows(step):
        def body(r, cc):
            step(rows(r * RB, RB, RB))
            return cc

        lax.fori_loop(0, ROWS // RB, body, 0)

    def reorder(a, src, dst):
        @pl.when(a == 2)
        def _():
            dst[...] = src[...]

        @pl.when(a != 2)
        def _():
            def step(at):
                dst[at, :] = mm(perm[jnp.minimum(a, 1), at, :], src[...]).astype(BF)

            by_rows(step)

    def dispatch(i, carry):
        @pl.when(i < 2 * NC)
        def _():
            buf = lax.rem(i, NS)
            a = axis(i)

            @pl.when(jnp.logical_and(i >= 1, i < 3))
            def _():
                build(a)

            await_once(tok.at[i], ag_sr.at[i], 4 * TOK)

            @pl.when(i >= NS)
            def _():
                await_sbuf(buf)

            def gather(at):
                sbuf[buf, at, :] = mm(gat[a, at, :], tok[i]).astype(BF)

            by_rows(gather)
            await_once(tok.at[i], ag_ss.at[i], 7 * TOK)
            spread(frame(a), buf, rcv.at[i], a_rs.at[i], a_self.at[i])

        @pl.when(i == 1)
        def _():
            saux[...] = mm(gat[2], tokaux[2]).astype(BF)
            mine = rows(zf.place() * MSG, MSG)
            for p, d in zf.peers():
                put(saux.at[rows(p * MSG, MSG)], raux.at[mine], x_ss.at[1], x_rs.at[2], d)
            pltpu.make_async_copy(saux.at[mine], raux.at[mine], x_self.at[0]).start()

        @pl.when(i >= LAG)
        def _():
            j = i - LAG
            await_spread(rcv.at[j], a_rs.at[j], a_self.at[j])

            @pl.when(j < NC)
            def _():
                reorder(axis(j), rcv.at[j], canon)
                wd_copy(j).wait()

                def step(at):
                    got = mm_nt(canon[at, :], wdb[lax.rem(j, 2)])

                    @pl.when(j == 0)
                    def _():
                        acc[2, at, :] = got

                    @pl.when(j > 0)
                    def _():
                        acc[2, at, :] += got

                by_rows(step)

                @pl.when(j + 2 < NC)
                def _():
                    wd_copy(j + 2).start()

            @pl.when(j >= NC)
            def _():
                n = j - NC
                reorder(axis(j), rcv.at[j], rcv.at[n])
                for cp in wgu_copies(n):
                    cp.wait()

                def step(at):
                    for m, w in ((0, wgb), (1, wub)):
                        got = mm(rcv[n, at, :], w[lax.rem(n, 2)])

                        @pl.when(n == 0)
                        def _():
                            acc[m, at, :] = got

                        @pl.when(n > 0)
                        def _():
                            acc[m, at, :] += got

                by_rows(step)
                for cp in wgu_copies(n + 2):
                    cp.start()

        @pl.when(i == 0)
        def _():
            for n in range(4, L2):
                ag_second(n)
            for n in range(6, L1):
                ag_first(n)

        @pl.when(i + L1 < 2 * NC)
        def _():
            ag_first(i + L1)

        @pl.when(i + L3 < 2 * NC)
        def _():
            ag_third(i + L3)

        @pl.when(i + L2 < 2 * NC)
        def _():
            ag_second(i + L2)

        return carry

    lax.fori_loop(0, 2 * NC - 1 + LAG, dispatch, 0)

    pl.semaphore_signal(free_sib, inc=1, device_id=sib, device_id_type=MESH)
    for a in range(3):
        for d in (1, 3):
            pl.semaphore_signal(free_ring, inc=1, device_id=frame(a).ring(d), device_id_type=MESH)

    await_once(raux, x_rs.at[2], 15 * MSG)
    await_once(raux, x_self.at[0], MSG)
    await_once(saux, x_ss.at[1], 15 * MSG)
    alane = lax.broadcasted_iota(jnp.int32, (AB, 128), 1)

    def activate(at):
        scale = jnp.sum(jnp.where(alane == me, raux[at, :].astype(F32), 0.0), axis=1, keepdims=True)
        comb = jnp.zeros((AB, 1), F32)
        for half in range(2):
            cols = slice(half * CW, (half + 1) * CW)
            gate, up, back = acc[0, at, cols], acc[1, at, cols], acc[2, at, cols]
            sig = jax.nn.sigmoid(gate)
            act = gate * sig
            comb = comb + jnp.sum(act * up * back, axis=1, keepdims=True)
            scaled = scale * back
            rcv[NC + half, at, :] = (scaled * up * sig * (1.0 + gate * (1.0 - sig))).astype(BF)
            rcv[NC + 2 + half, at, :] = (scaled * act).astype(BF)
        caux[at, :] = jnp.where(alane == me, comb, 0.0).astype(BF)

    def slot_rows(at, n):
        b = lax.rem(n, 2)
        got = mm_nt(rcv[NC, at, :], wgb[b, :, 0:CW])
        got = got + mm_nt(rcv[NC + 1, at, :], wgb[b, :, CW:H])
        got = got + mm_nt(rcv[NC + 2, at, :], wub[b, :, 0:CW])
        got = got + mm_nt(rcv[NC + 3, at, :], wub[b, :, CW:H])
        return got.astype(BF)

    def gain_sum(cut, k, at):
        return jnp.sum(cut.astype(F32) * rcv[k, at, :].astype(F32), axis=0, keepdims=True)

    QB = 4 * MSG
    LAST = 2 * NC - 1
    first_buf = (2 * NC) % NS
    await_spread(rcv.at[LAST], a_rs.at[LAST], a_self.at[LAST])
    for n in (NC - 1, NC):
        for cp in wgu_copies(n):
            cp.wait()
    await_sbuf(first_buf)
    z_mine = rows(zf.place() * MSG, MSG)

    def turn_round(t, gsum):
        du = lax.rem(t + 1, 4)
        u = lax.rem(zf.u + du, 4)
        at = rows(u * QB, QB)
        got = rcv[LAST, at, :]
        rcv[NC - 1, at, :] = got
        acc[0, at, :] += mm(got, wgb[(NC - 1) % 2])
        acc[1, at, :] += mm(got, wub[(NC - 1) % 2])
        for r in range(QB // AB):
            activate(rows(u * QB + r * AB, AB))
        cut = slot_rows(at, NC)
        sbuf[first_buf, at, :] = cut
        for dv in range(4):
            v = lax.rem(zf.v + dv, 4)
            src = sbuf.at[first_buf, rows((u * 4 + v) * MSG, MSG)]
            to = device(*zf.coords(u, v, zf.r), c)
            if dv:
                put(src, tok.at[0, z_mine], a_ss.at[first_buf], r_rs.at[0], to)
            else:

                @pl.when(du != 0)
                def _():
                    put(src, tok.at[0, z_mine], a_ss.at[first_buf], r_rs.at[0], to)

                @pl.when(du == 0)
                def _():
                    pltpu.make_async_copy(src, tok.at[0, z_mine], r_self.at[0]).start()

        return gsum + gain_sum(cut, 0, at)

    gstage[:, 0:CW] = lax.fori_loop(0, 4, turn_round, jnp.zeros((1, CW), F32))
    for n in (NC + 1, NC + 2):
        for cp in wgu_copies(n):
            cp.start()

    half_me, half_sib = rows(c * 512, 512, 512), rows((1 - c) * 512, 512, 512)

    def col_half(k):
        return pl.ds(pl.multiple_of(lax.rem(k, 2) * CW, CW), CW)

    def own_part(k):
        return 2 * lax.div(lax.rem(k, 4), 2)

    def grad_rows(k):
        return rows(lax.div(k, 2) * TOK, TOK, TOK)

    def send_back(i):
        n = i + NC
        a = back_axis(i)
        buf = lax.rem(i + 2 * NC, NS)
        for cp in wgu_copies(n):
            cp.wait()

        def step(r, gsum):
            at = rows(r * RB, RB, RB)
            cut = slot_rows(at, n)
            canon[at, :] = cut
            return gsum + gain_sum(cut, i, at)

        gsum = lax.fori_loop(0, ROWS // RB, step, jnp.zeros((1, CW), F32))
        gstage[:, pl.ds(pl.multiple_of(i * CW, CW), CW)] = gsum
        await_sbuf(buf)
        reorder(a, canon, sbuf.at[buf])
        spread(frame(a), buf, tok.at[i], r_rs.at[i], r_self.at[i])

        @pl.when(i + 2 < NC)
        def _():
            for cp in wgu_copies(n + 2):
                cp.start()

    def combine(k):
        b = lax.rem(k, 2)
        a = back_axis(k)
        await_spread(tok.at[k], r_rs.at[k], r_self.at[k])

        @pl.when(k >= 2)
        def _():
            await_bytes(pbuf.at[b], p_ss.at[b])

        pbuf[b] = mm(gatt[a, half_sib, :], tok[k, 0:ROWS, :]).astype(BF)
        put(pbuf.at[b], tok.at[NC + k, pl.ds(0, 512)], p_ss.at[b], p_rs.at[k], sib)
        acc[own_part(k), 0:512, col_half(k)] = mm(gatt[a, half_me, :], tok[k, 0:ROWS, :])

    def both_cores(k, f, d):
        at = rows(((f.r + d) % 4) * TOK, TOK, TOK)
        return acc[own_part(k), at, col_half(k)] + tok[NC + k, at, :].astype(F32)

    def relay(k):
        b = lax.rem(k, 2)
        f = frame(back_axis(k))
        await_bytes(tok.at[NC + k, pl.ds(0, 512)], p_rs.at[k])

        @pl.when(k >= 2)
        def _():
            await_bytes(q1buf.at[b], q1_ss.at[b])

        q1buf[b] = both_cores(k, f, 2).astype(BF)
        for d, part in ((1, 0), (3, HALF)):
            put(
                q1buf.at[b, pl.ds(part, HALF)], tok.at[NC + k, pl.ds(512 + part, HALF)],
                q1_ss.at[b], q1_rs.at[k], f.ring(d),
            )

    def scatter(k):
        b = lax.rem(k, 2)
        f = frame(back_axis(k))
        await_bytes(tok.at[NC + k, pl.ds(512, TOK)], q1_rs.at[k])

        @pl.when(k >= 2)
        def _():
            await_bytes(q2buf.at[b], q2_ss.at[b])

        on = both_cores(k, f, 1)
        q2buf[b, 0:HALF, :] = (on[0:HALF] + tok[NC + k, 512 : 512 + HALF, :].astype(F32)).astype(BF)
        q2buf[b, HALF:TOK, :] = on[HALF:TOK].astype(BF)
        on = both_cores(k, f, 3)
        q2buf[b, TOK : TOK + HALF, :] = on[0:HALF].astype(BF)
        q2buf[b, TOK + HALF : 2 * TOK, :] = (
            on[HALF:TOK] + tok[NC + k, 512 + HALF : 512 + TOK, :].astype(F32)
        ).astype(BF)
        for d, part in ((1, 0), (3, TOK)):
            put(
                q2buf.at[b, pl.ds(part, TOK)], tok.at[NC + k, pl.ds(640 + part, TOK)],
                q2_ss.at[b], q2_rs.at[k], f.ring(d),
            )
        acc[1, grad_rows(k), col_half(k)] = both_cores(k, f, 0)

    def settle(k):
        await_bytes(tok.at[NC + k, pl.ds(640, 2 * TOK)], q2_rs.at[k])
        grad = acc[1, grad_rows(k), col_half(k)]
        for d in range(2):
            grad = grad + tok[NC + k, 640 + d * TOK : 640 + (d + 1) * TOK, :].astype(F32)
        cols = pl.ds(pl.multiple_of(k * CW, CW), CW)
        scaled = grad * gain[:, cols]
        acc[1, grad_rows(k), col_half(k)] = scaled
        proj_s[...] += scaled * (hid[:, cols].astype(F32) * inv_s[:, 0:1])

    proj_s[...] = jnp.zeros_like(proj_s)

    def back(i, carry):
        @pl.when(i == K1)
        def _():
            pl.semaphore_wait(free_sib, 1)
            pl.semaphore_wait(free_ring, 6)

        @pl.when(jnp.logical_and(i >= 1, i < NC))
        def _():
            send_back(i)

        @pl.when(i >= K4)
        def _():
            settle(i - K4)

        @pl.when(jnp.logical_and(i >= K3, i < NC + K3))
        def _():
            scatter(i - K3)

        @pl.when(jnp.logical_and(i >= K2, i < NC + K2))
        def _():
            relay(i - K2)

        @pl.when(jnp.logical_and(i >= K1, i < NC + K1))
        def _():
            combine(i - K1)

        @pl.when(i == 0)
        def _():
            mine = rows(zf.place() * MSG, MSG)
            for p, d in zf.peers():
                put(caux.at[rows(p * MSG, MSG)], cret.at[mine], x_ss.at[2], x_rs.at[3], d)
            pltpu.make_async_copy(caux.at[mine], cret.at[mine], x_self.at[1]).start()

        @pl.when(i == 3)
        def _():
            await_once(cret, x_rs.at[3], 15 * MSG)
            await_once(cret, x_self.at[1], MSG)
            await_once(caux, x_ss.at[2], 15 * MSG)
            paux[...] = mm(gatt[2, half_sib, :], cret[...]).astype(BF)
            put(paux, sibaux, x_ss.at[3], x_rs.at[4], sib)

        @pl.when(i == 5)
        def _():
            await_bytes(sibaux, x_rs.at[4])
            await_bytes(paux, x_ss.at[3])
            qaux[...] = (mm(gatt[2, half_me, :], cret[...]) + sibaux[...].astype(F32)).astype(BF)
            for d in (1, 2, 3):
                at = rows(((z + d) % 4) * TOK, TOK, TOK)
                put(qaux.at[at], ringaux.at[pl.ds((d - 1) * TOK, TOK)], x_ss.at[4], x_rs.at[5], zf.ring(d))

        @pl.when(i == NC - 1)
        def _():
            gall[zf.place()] = gstage[...]
            for _, d in zf.peers():
                put(gall.at[zf.place()], gall.at[zf.place()], g_ss.at[0], g_rs.at[0], d)

        @pl.when(i == NC)
        def _():
            await_once(gall, g_rs.at[0], 15)
            await_once(gall, g_ss.at[0], 15)
            gring[z] = jnp.sum(gall[...], axis=0)
            for d in (1, 2, 3):
                put(gring.at[z], gring.at[z], g_ss.at[1], g_rs.at[1], zf.ring(d))

        @pl.when(i == NC + 1)
        def _():
            await_once(gring, g_rs.at[1], 3)
            await_once(gring, g_ss.at[1], 3)
            gsib[c] = gring[0] + gring[1] + gring[2] + gring[3]
            put(gsib.at[c], gsib.at[c], g_ss.at[2], g_rs.at[2], sib)

        return carry

    lax.fori_loop(0, NC + K4, back, 0)

    project = jnp.sum(proj_s[...], axis=1, keepdims=True) * (1.0 / D)
    inv = inv_s[:, 0:1]
    for k in range(NC):
        cols = slice(k * CW, (k + 1) * CW)
        scaled = acc[1, (k // 2) * TOK : (k // 2 + 1) * TOK, (k % 2) * CW : (k % 2 + 1) * CW]
        unit = hid[:, cols].astype(F32) * inv
        out_ref[:, cols] = (inv * (scaled - unit * project)).astype(BF)

    await_once(gsib, g_rs.at[2], 1)
    await_once(gsib, g_ss.at[2], 1)
    for r in range(D // 128):
        cols = slice(r * 128, (r + 1) * 128)
        gout_ref[r : r + 1, :] = (gsib[0, :, cols] + gsib[1, :, cols]) / gain[:, cols]

    await_bytes(ringaux, x_rs.at[5])
    await_bytes(ringaux, x_ss.at[4])
    cfin = qaux[rows(z * TOK, TOK, TOK), :].astype(F32)
    for d in range(3):
        cfin = cfin + ringaux[d * TOK : (d + 1) * TOK, :].astype(F32)
    picked = jnp.zeros((TOK, 128), F32)
    named_by = jnp.transpose(turn[...])
    for k in range(4):
        got = jnp.sum(jnp.where(named_by[:, k : k + 1] == lane_f, cfin, 0.0), axis=1, keepdims=True)
        picked = jnp.where(lane == k, got, picked)
    cout_ref[...] = jnp.transpose(picked)[0:4, :].astype(BF)

    for b in range(NS):
        await_sbuf(b)
    for b in range(2):
        await_bytes(pbuf.at[b], p_ss.at[b])
        await_bytes(q1buf.at[b], q1_ss.at[b])
        await_bytes(q2buf.at[b], q2_ss.at[b])


def hand_over(*refs):
    for src, dst in zip(refs[0:3], refs[3:6]):
        dst[...] = src[...]


def shards(hidden_in, norm_gain, upstream, routes, combine_fixed, w_gate, w_up, w_down):
    vm = pl.BlockSpec(memory_space=pltpu.VMEM)
    hbm = pl.BlockSpec(memory_space=pl.ANY)
    dma = pltpu.SemaphoreType.DMA
    shapes = (
        jax.ShapeDtypeStruct((TOK, D), BF),
        jax.ShapeDtypeStruct((D // 128, 128), F32),
        jax.ShapeDtypeStruct((4, TOK), BF),
    )
    results = pl.pallas_call(
        kernel,
        out_shape=shapes,
        in_specs=[hbm, vm, hbm, vm, vm, hbm, hbm, hbm],
        out_specs=(vm, vm, vm),
        scratch_shapes=[
            pltpu.VMEM((2 * NC, GTOK, CW), BF),
            pltpu.VMEM((3, GTOK, 128), BF),
            pltpu.VMEM((3, ROWS, GTOK), BF),
            pltpu.VMEM((3, GTOK, ROWS), BF),
            pltpu.VMEM((2, ROWS, ROWS), BF),
            pltpu.VMEM((NS, ROWS, CW), BF),
            pltpu.VMEM((ROWS, 128), BF),
            pltpu.VMEM((2 * NC, ROWS, CW), BF),
            pltpu.VMEM((ROWS, 128), BF),
            pltpu.VMEM((ROWS, CW), BF),
            pltpu.VMEM((3, ROWS, H), F32),
            pltpu.VMEM((TOK, D), BF),
            pltpu.VMEM((1, D), F32),
            pltpu.VMEM((8, TOK), F32),
            pltpu.VMEM((2, H, CW), BF),
            pltpu.VMEM((2, CW, H), BF),
            pltpu.VMEM((2, CW, H), BF),
            pltpu.VMEM((ROWS, 128), BF),
            pltpu.VMEM((ROWS, 128), BF),
            pltpu.VMEM((2, 512, CW), BF),
            pltpu.VMEM((512, 128), BF),
            pltpu.VMEM((2, TOK, CW), BF),
            pltpu.VMEM((2, 2 * TOK, CW), BF),
            pltpu.VMEM((512, 128), BF),
            pltpu.VMEM((512, 128), BF),
            pltpu.VMEM((384, 128), BF),
            pltpu.VMEM((TOK, 128), F32),
            pltpu.VMEM((TOK, CW), F32),
            pltpu.VMEM((16, 1, D), F32),
            pltpu.VMEM((4, 1, D), F32),
            pltpu.VMEM((2, 1, D), F32),
            pltpu.VMEM((1, D), F32),
            dma((2,)),
            dma((3, 2)),
            dma((2 * NC,)),
            dma((2 * NC,)),
            dma((2 * NC,)),
            dma((2 * NC,)),
            dma((3,)),
            dma((3,)),
            dma((3,)),
            dma((NS,)),
            dma((2 * NC,)),
            dma((2 * NC,)),
            dma((5,)),
            dma((6,)),
            dma((2,)),
            dma((NC,)),
            dma((NC,)),
            dma((2,)),
            dma((NC,)),
            dma((2,)),
            dma((NC,)),
            dma((2,)),
            dma((NC,)),
            dma((3,)),
            dma((3,)),
            pltpu.SemaphoreType.REGULAR,
            pltpu.SemaphoreType.REGULAR,
        ],
        compiler_params=pltpu.CompilerParams(
            collective_id=0, has_side_effects=True, vmem_limit_bytes=63 * 2**20
        ),
        cost_estimate=pl.CostEstimate(flops=50 * 10**9, bytes_accessed=40 * 10**6, transcendentals=10**6),
    )(hidden_in, norm_gain.reshape(D // 128, 128), upstream, routes.T, combine_fixed.T, w_gate, w_up, w_down)
    out, gain_grad, combine_grad = pl.pallas_call(
        hand_over,
        out_shape=shapes,
        in_specs=[vm] * 3,
        out_specs=(vm,) * 3,
    )(*results)
    return out, gain_grad.reshape(D), combine_grad.T


def solution(mesh):
    split = ("expert", "tensor")
    in_specs = (
        P(split, None),
        P(),
        P(split, None),
        P(split, None),
        P(split, None),
        P(split, None, None),
        P(split, None, None),
        P(split, None, None),
    )
    out_specs = (P(split, None), P(), P(split, None))
    return jax.shard_map(shards, mesh=mesh, in_specs=in_specs, out_specs=out_specs, check_vma=False)
```

time: 247 us -> 224 us (0.907)
  Pallas kernels: 237 us -> 222 us
  local copies, waits for them, and re-layouts: 7.71 us -> 0 us
    pallas_call x1 -> x2, Pallas kernels: 237 us -> 222 us  [the longest x1 220 us: shards(): pl.pallas_call(kernel, out_shape=shapes, in_specs=[hbm, vm, hbm, vm, vm,...]
    unnamed x4 -> x0, local copies, waits for them, and re-layouts: 6.38 us -> none
where the time goes in v2:
time: 224 us; the launch traced here: 223 us
  Pallas kernels  222 us (99%)
    pallas_call x1, Pallas kernels, shards(): pl.pallas_call(kernel, out_shape=shapes, in_specs=[hbm, vm, hbm, vm, vm,...  220 us

profile of v2, /device:TPU:0, one launch (start us, length us, event | category | flops | bytes accessed | tf_op | source)
XLA Modules:
  0.0 222.7 jit_solution(8188462708967208687)
XLA Ops:
  0.6 219.9 %shard_map.103 = (bf16[128,3584]{1,0:T(8,128)(2,1)}, f32[28,128]{1,0:T(8,128)}, bf16[4,128]{1,0:T(4,128)(2,1)}) custom-call(bf16[128,3584]{1,0:T(8,128)(2,1)} %hid_ref.1, f32[28,128]{1,0:T(8,128)} %bitcast.5, bf16[128,3584]{1,0:T(8,128)(2,1)} %ups_ref.1, s32[4,128]{1,0:T(4,128)} %bitcast.7, s32[4,128]{1,0:T(4,128)} %bitcast.8, ...), custom_call_target="tpu_custom_call" | custom-call | flops 49999998976 | bytes 40000000 | tf_op jit(solution)/shard_map/pallas_call | solution.py:714
  220.5 2.2 shard_map.104

commit v3 on v2

--- a/solution.py
+++ b/solution.py
@@ -23,12 +23,12 @@
 RB = 256
 AB = 64
 L1, L2, L3 = 7, 5, 3
-K1, K2, K3, K4 = 2, 4, 5, 7
+K1, K2, K3, K4 = 2, 4, 6, 8
 LAG = 3
 
 
 def device(x, y, z, c):
-    return {"expert": (y // 2) * 4 + x, "tensor": z * 4 + (y % 2) * 2 + c}
+    return {"expert": lax.div(y, 2) * 4 + x, "tensor": z * 4 + lax.rem(y, 2) * 2 + c}
 
 
 def mm(a, b):
@@ -45,9 +45,9 @@
 
 class Frame:
     def __init__(self, a, x, y, z, c):
-        self.is0 = (a - 1) * (a - 2) // 2
+        self.is0 = (a - 1) * (a - 2) // 2 if isinstance(a, int) else lax.div((a - 1) * (a - 2), 2)
         self.is1 = a * (2 - a)
-        self.is2 = a * (a - 1) // 2
+        self.is2 = a * (a - 1) // 2 if isinstance(a, int) else lax.div(a * (a - 1), 2)
         self.u = (1 - self.is1) * y + self.is1 * z
         self.v = (1 - self.is0) * x + self.is0 * z
         self.r = self.is2 * z + self.is0 * x + self.is1 * y
@@ -61,11 +61,11 @@
         )
 
     def ring(self, d):
-        return device(*self.coords(self.u, self.v, (self.r + d) % 4), self.c)
+        return device(*self.coords(self.u, self.v, lax.rem(self.r + d, 4)), self.c)
 
     def peers(self):
         for dv, du in PLANE:
-            u, v = (self.u + du) % 4, (self.v + dv) % 4
+            u, v = lax.rem(self.u + du, 4), lax.rem(self.v + dv, 4)
             yield u * 4 + v, device(*self.coords(u, v, self.r), self.c)
 
     def place(self):
@@ -82,7 +82,8 @@
     r_rs, r_self, p_ss, p_rs, q1_ss, q1_rs, q2_ss, q2_rs, g_ss, g_rs, free_sib, free_ring,
 ):
     e_i, t_i = lax.axis_index("expert"), lax.axis_index("tensor")
-    x, y, z, c = e_i % 4, (e_i // 4) * 2 + (t_i // 2) % 2, t_i // 4, t_i % 2
+    x, y = lax.rem(e_i, 4), lax.div(e_i, 4) * 2 + lax.rem(lax.div(t_i, 2), 2)
+    z, c = lax.div(t_i, 4), lax.rem(t_i, 2)
     me = e_i * 16 + t_i
     sib = device(x, y, z, 1 - c)
 
@@ -99,7 +100,7 @@
         return rows((c * 4 + f.r) * TOK, TOK, TOK)
 
     def ring_rows(f, d):
-        return rows((c * 4 + (f.r + d) % 4) * TOK, TOK, TOK)
+        return rows((c * 4 + lax.rem(f.r + d, 4)) * TOK, TOK, TOK)
 
     def put(src, dst, ss, rs, to):
         pltpu.make_async_remote_copy(
@@ -119,7 +120,7 @@
         for dy in range(4):
             for dz in range(4):
                 if 0 in (dx, dy, dz) and (dx or dy or dz):
-                    everyone.append(device((x + dx) % 4, (y + dy) % 4, (z + dz) % 4, c))
+                    everyone.append(device(lax.rem(x + dx, 4), lax.rem(y + dy, 4), lax.rem(z + dz, 4), c))
     for d in everyone:
         pl.semaphore_signal(bar, inc=1, device_id=d, device_id_type=MESH)
 
@@ -131,14 +132,14 @@
 
     def wd_copy(n):
         return pltpu.make_async_copy(
-            wd_ref.at[0, :, pl.ds(pl.multiple_of(n * CW, CW), CW)], wdb.at[n % 2], w_sem.at[0, n % 2]
+            wd_ref.at[0, :, pl.ds(pl.multiple_of(n * CW, CW), CW)], wdb.at[lax.rem(n, 2)], w_sem.at[0, lax.rem(n, 2)]
         )
 
     def wgu_copies(n):
         at = rows(jnp.where(n >= NC, n - NC, n) * CW, CW, CW)
         return (
-            pltpu.make_async_copy(wg_ref.at[0, at], wgb.at[n % 2], w_sem.at[1, n % 2]),
-            pltpu.make_async_copy(wu_ref.at[0, at], wub.at[n % 2], w_sem.at[2, n % 2]),
+            pltpu.make_async_copy(wg_ref.at[0, at], wgb.at[lax.rem(n, 2)], w_sem.at[1, lax.rem(n, 2)]),
+            pltpu.make_async_copy(wu_ref.at[0, at], wub.at[lax.rem(n, 2)], w_sem.at[2, lax.rem(n, 2)]),
         )
 
     for n in (0, 1):
@@ -180,7 +181,7 @@
         f = frame(axis(i))
         await_once(tok.at[i], ag_r1.at[i], 2 * TOK)
         for d, part in ((3, 0), (1, HALF)):
-            at = rows((c * 4 + (f.r + d) % 4) * TOK + part, HALF, HALF)
+            at = rows((c * 4 + lax.rem(f.r + d, 4)) * TOK + part, HALF, HALF)
             put(tok.at[i, at], tok.at[i, at], ag_ss.at[i], ag_r2.at[i], f.ring(4 - d))
         for d in (3, 1):
             at = ring_rows(f, d)
@@ -260,11 +261,11 @@
             put(tokaux.at[a, at], tokaux.at[a, at], aux_ss.at[a], aux_s.at[a], sib)
     for i in range(3):
         ag_second(i)
-    for i in range(3, 6):
-        ag_first(i)
     build(1)
     for i in range(3):
         ag_third(i)
+    for i in range(3, 6):
+        ag_first(i)
     swaps()
     ag_second(3)
 
@@ -533,7 +534,7 @@
         acc[own_part(k), 0:512, col_half(k)] = mm(gatt[a, half_me, :], tok[k, 0:ROWS, :])
 
     def both_cores(k, f, d):
-        at = rows(((f.r + d) % 4) * TOK, TOK, TOK)
+        at = rows(lax.rem(f.r + d, 4) * TOK, TOK, TOK)
         return acc[own_part(k), at, col_half(k)] + tok[NC + k, at, :].astype(F32)
 
     def relay(k):

time: 224 us -> 207 us (0.924)
  Pallas kernels: 222 us -> 206 us
    pallas_call x1, Pallas kernels: 220 us -> 204 us  [shards(): pl.pallas_call(kernel, out_shape=shapes, in_specs=[hbm, vm, hbm, vm, vm,...]
where the time goes in v3:
time: 207 us
  Pallas kernels  206 us (100%)
    pallas_call x1, Pallas kernels, shards(): pl.pallas_call(kernel, out_shape=shapes, in_specs=[hbm, vm, hbm, vm, vm,...  204 us

profile of v3, /device:TPU:0, one launch (start us, length us, event | category | flops | bytes accessed | tf_op | source)
XLA Modules:
  0.0 206.8 jit_solution(15075762289301094388)
XLA Ops:
  0.6 203.9 %shard_map.103 = (bf16[128,3584]{1,0:T(8,128)(2,1)}, f32[28,128]{1,0:T(8,128)}, bf16[4,128]{1,0:T(4,128)(2,1)}) custom-call(bf16[128,3584]{1,0:T(8,128)(2,1)} %hid_ref.1, f32[28,128]{1,0:T(8,128)} %bitcast.5, bf16[128,3584]{1,0:T(8,128)(2,1)} %ups_ref.1, s32[4,128]{1,0:T(4,128)} %bitcast.7, s32[4,128]{1,0:T(4,128)} %bitcast.8, ...), custom_call_target="tpu_custom_call" | custom-call | flops 49999998976 | bytes 40000000 | tf_op jit(solution)/shard_map/pallas_call | solution.py:715
  204.6 2.2 %shard_map.104 = (bf16[128,3584]{1,0:T(8,128)(2,1)}, f32[28,128]{1,0:T(8,128)}, bf16[4,128]{1,0:T(4,128)(2,1)}) custom-call(bf16[128,3584]{1,0:T(8,128)(2,1)} %get-tuple-element.9.refs_0_, f32[28,128]{1,0:T(8,128)} %get-tuple-element.10.refs_1_, bf16[4,128]{1,0:T(4,128)(2,1)} %get-tuple-element.11.refs_2_), custom_call_target="tpu_custom_call" | custom-call | tf_op jit(solution)/shard_map/pallas_call | solution.py:786

commit v4 on v3

--- a/solution.py
+++ b/solution.py
@@ -599,10 +599,6 @@
         def _():
             send_back(i)
 
-        @pl.when(i >= K4)
-        def _():
-            settle(i - K4)
-
         @pl.when(jnp.logical_and(i >= K3, i < NC + K3))
         def _():
             scatter(i - K3)
@@ -659,6 +655,10 @@
             await_once(gring, g_ss.at[1], 3)
             gsib[c] = gring[0] + gring[1] + gring[2] + gring[3]
             put(gsib.at[c], gsib.at[c], g_ss.at[2], g_rs.at[2], sib)
+
+        @pl.when(i >= K4)
+        def _():
+            settle(i - K4)
 
         return carry
 

time: 207 us -> 207 us (level)
  no operation moved by 1% of the time
where the time goes in v4:
time: 207 us
  Pallas kernels  206 us (100%)
    pallas_call x1, Pallas kernels, shards(): pl.pallas_call(kernel, out_shape=shapes, in_specs=[hbm, vm, hbm, vm, vm,...  204 us

profile of v4, /device:TPU:0, one launch (start us, length us, event | category | flops | bytes accessed | tf_op | source)
XLA Modules:
  0.0 206.7 jit_solution(13764420632463564146)
XLA Ops:
  0.6 203.9 %shard_map.103 = (bf16[128,3584]{1,0:T(8,128)(2,1)}, f32[28,128]{1,0:T(8,128)}, bf16[4,128]{1,0:T(4,128)(2,1)}) custom-call(bf16[128,3584]{1,0:T(8,128)(2,1)} %hid_ref.1, f32[28,128]{1,0:T(8,128)} %bitcast.5, bf16[128,3584]{1,0:T(8,128)(2,1)} %ups_ref.1, s32[4,128]{1,0:T(4,128)} %bitcast.7, s32[4,128]{1,0:T(4,128)} %bitcast.8, ...), custom_call_target="tpu_custom_call" | custom-call | flops 49999998976 | bytes 40000000 | tf_op jit(solution)/shard_map/pallas_call | solution.py:715
  204.5 2.2 %shard_map.104 = (bf16[128,3584]{1,0:T(8,128)(2,1)}, f32[28,128]{1,0:T(8,128)}, bf16[4,128]{1,0:T(4,128)(2,1)}) custom-call(bf16[128,3584]{1,0:T(8,128)(2,1)} %get-tuple-element.9.refs_0_, f32[28,128]{1,0:T(8,128)} %get-tuple-element.10.refs_1_, bf16[4,128]{1,0:T(4,128)(2,1)} %get-tuple-element.11.refs_2_), custom_call_target="tpu_custom_call" | custom-call | tf_op jit(solution)/shard_map/pallas_call | solution.py:786
